TPU v7x, 256 devices: a whole 4x4x8 slice. The times are simulated.
256 devices in a mesh: ctx: 32 (over x, z_lo, core), tp: 8 (over z_hi, y).
Axes of the slice: x: 4, y: 4, z: 8 (z_hi: 2, z_lo: 4; z = z_hi * 4 + z_lo), core: 2. Of those that a mesh axis runs over, the one named last changes fastest.
Arguments:
- q_nope: bfloat16 [4096, 128, 128], P('ctx', 'tp'), may hold values from -6 to 6
- q_rope: bfloat16 [4096, 8192], P('ctx', 'tp'), may hold values from -8 to 8
- latent: bfloat16 [4096, 512], P('ctx'), may hold values from -6 to 6
- k_rope: bfloat16 [4096, 64], P('ctx'), may hold values from -8 to 8
- out_grad: bfloat16 [4096, 128, 128], P('ctx', 'tp'), may hold values from -6 to 6
- w_key: bfloat16 [128, 128, 512], P('tp'), may hold values from -0.25 to 0.25
- w_value: bfloat16 [128, 512, 128], P('tp'), may hold values from -0.25 to 0.25
- lengths: int32 [6], replicated, may hold values from 1 to 768, 4096 in all
Outputs:
- grad_q_nope: bfloat16 [4096, 128, 128], P('ctx', 'tp')
- grad_q_rope: bfloat16 [4096, 8192], P('ctx', 'tp')
- grad_latent: bfloat16 [4096, 512], P('ctx')
- grad_k_rope: bfloat16 [4096, 64], P('ctx')
- grad_w_key: bfloat16 [128, 128, 512], P('tp', 'ctx')
- grad_w_value: bfloat16 [128, 512, 128], P('tp', 'ctx')
Inputs may be any that keep to these rules, and one draw needn't show every extreme that they name: `lengths`: every document has 1 to 768 tokens, one exactly 768, and they sum to 4096.
All inputs are finite; a program needn't handle non-finite values.
Results may differ from a plain program's by a relative error of at most 0.034.
Values may be sent and summed in bfloat16 or wider, within the bound.
A program may use at most 192 MiB of HBM per device.

v0:
```python
import jax
import jax.numpy as jnp
from jax import lax
from jax.sharding import PartitionSpec as P

NOPE = 128
ROPE = 64
LATENT = 512
SPAN = 6


def passed_along(block, axis, distance):
    devices = range(lax.axis_size(axis))
    route = [(i - distance, i) for i in devices if i - distance in devices]
    return lax.ppermute(block, axis, route)


def shortened(shard):

    def short(part):
        return part.astype(jnp.bfloat16) if part.dtype == jnp.float32 else part

    return jax.tree.map(short, shard)


def doc_starts(lengths, positions):
    ends = jnp.cumsum(lengths)
    begins = ends - lengths
    inside = (begins[None, :] <= positions[:, None]) & (positions[:, None] < ends[None, :])
    return jnp.sum(jnp.where(inside, begins[None, :], 0), axis=1)


def per_device(q_nope, q_rope, latent, k_rope, out_grad, w_key, w_value, lengths):
    tok_rows = q_nope.shape[0]
    head_count = q_nope.shape[1]
    softmax_scale = float(NOPE + ROPE) ** (-0.5)
    shard_index = lax.axis_index("ctx")
    query_pos = shard_index * tok_rows + jnp.arange(tok_rows, dtype=jnp.int32)
    doc_start = doc_starts(lengths, query_pos)
    query_rope = q_rope.reshape(tok_rows, head_count, ROPE)
    blocks = [(latent, k_rope)]
    for distance in range(1, SPAN + 1):
        blocks.append(passed_along((latent, k_rope), "ctx", distance))
    ordered = blocks[::-1]
    lat_query = jnp.einsum(
        "thn,hnl->thl", q_nope, w_key, preferred_element_type=jnp.float32
    ).astype(jnp.bfloat16)
    grad_lat_out = jnp.einsum(
        "thn,hln->thl", out_grad, w_value, preferred_element_type=jnp.float32
    ).astype(jnp.bfloat16)
    key_sets = []
    key_lat = jnp.concatenate([pair[0] for pair in ordered], 0)
    key_rope = jnp.concatenate([pair[1] for pair in ordered], 0)
    key_pos = (shard_index - SPAN) * tok_rows + jnp.arange((SPAN + 1) * tok_rows, dtype=jnp.int32)
    allowed = (key_pos[None, :] >= doc_start[:, None]) & (key_pos[None, :] <= query_pos[:, None])
    key_sets.append((key_lat, key_rope, allowed, None))
    key_lat, key_rope, allowed, active = key_sets[0]
    width = key_lat.shape[0]

    def raw_scores(key_lat=key_lat, key_rope=key_rope):
        return softmax_scale * (
            jnp.einsum("thl,kl->htk", lat_query, key_lat, preferred_element_type=jnp.float32)
            + jnp.einsum("thr,kr->htk", query_rope, key_rope, preferred_element_type=jnp.float32)
        )

    raw = raw_scores()
    all_scores = [jnp.where(allowed[None], raw, -jnp.inf)]
    row_max = all_scores[0].max(axis=-1)
    scores = all_scores[0]
    total = jnp.sum(jnp.exp(scores - row_max[..., None]), axis=-1)
    log_total = row_max + jnp.log(total)
    all_probs = [jnp.exp(scores - log_total[..., None]) for scores in all_scores]
    all_prob16 = [prob.astype(jnp.bfloat16) for prob in all_probs]
    out_acc = jnp.zeros((tok_rows, head_count, LATENT), jnp.float32)
    for (key_lat, key_rope, allowed, active), prob16 in zip(key_sets, all_prob16):

        def weighted(key_lat=key_lat, prob16=prob16):
            return jnp.einsum("htk,kl->thl", prob16, key_lat, preferred_element_type=jnp.float32)

        out_acc = weighted()
    out_lat = out_acc.astype(jnp.bfloat16)
    grad_wvalue = jnp.einsum("thl,thn->hln", out_lat, out_grad, preferred_element_type=jnp.float32)
    correction = jnp.sum(out_lat.astype(jnp.float32) * grad_lat_out.astype(jnp.float32), axis=-1).T
    query_acc = jnp.zeros((tok_rows, head_count, LATENT), jnp.float32)
    rope_acc = jnp.zeros((tok_rows, head_count, ROPE), jnp.float32)
    key_terms = []
    for (key_lat, key_rope, allowed, active), prob, prob16 in zip(key_sets, all_probs, all_prob16):
        width = key_lat.shape[0]

        def backward_terms(key_lat=key_lat, key_rope=key_rope, prob=prob, prob16=prob16):
            grad_prob = jnp.einsum(
                "thl,kl->htk", grad_lat_out, key_lat, preferred_element_type=jnp.float32
            )
            grad_scores = (softmax_scale * prob * (grad_prob - correction[..., None])).astype(
                jnp.bfloat16
            )
            part_query = jnp.einsum(
                "htk,kl->thl", grad_scores, key_lat, preferred_element_type=jnp.float32
            )
            part_rope = jnp.einsum(
                "htk,kr->thr", grad_scores, key_rope, preferred_element_type=jnp.float32
            )
            part_keys = jnp.einsum(
                "htk,thl->kl", grad_scores, lat_query, preferred_element_type=jnp.float32
            ) + jnp.einsum("htk,thl->kl", prob16, grad_lat_out, preferred_element_type=jnp.float32)
            part_krope = jnp.einsum(
                "htk,thr->kr", grad_scores, query_rope, preferred_element_type=jnp.float32
            )
            return (part_query, part_rope, part_keys, part_krope)

        part_query, part_rope, part_keys, part_krope = backward_terms()
        query_acc = part_query
        rope_acc = part_rope
        for index in range(width // tok_rows):
            key_terms.append(
                (
                    part_keys[index * tok_rows : (index + 1) * tok_rows],
                    part_krope[index * tok_rows : (index + 1) * tok_rows],
                )
            )
    grad_lat_query = query_acc.astype(jnp.bfloat16)
    grad_q_rope = rope_acc.astype(jnp.bfloat16).reshape(tok_rows, head_count * ROPE)
    grad_q_nope = jnp.einsum(
        "thl,hnl->thn", grad_lat_query, w_key, preferred_element_type=jnp.float32
    ).astype(jnp.bfloat16)
    grad_wkey = jnp.einsum(
        "thn,thl->hnl", q_nope, grad_lat_query, preferred_element_type=jnp.float32
    )
    by_distance = key_terms[::-1]
    lat_total, rope_total = by_distance[0]
    for distance in range(1, SPAN + 1):
        arrived = passed_along(shortened(by_distance[distance]), "ctx", -distance)
        lat_total = lat_total + arrived[0]
        rope_total = rope_total + arrived[1]
    lat_sum, rope_sum = (
        lax.psum(lat_total.astype(jnp.bfloat16), "tp").astype(jnp.float32),
        lax.psum(rope_total.astype(jnp.bfloat16), "tp").astype(jnp.float32),
    )
    wkey_share, wvalue_share = (
        lax.psum_scatter(
            grad_wkey.astype(jnp.bfloat16), "ctx", scatter_dimension=1, tiled=True
        ).astype(jnp.float32),
        lax.psum_scatter(
            grad_wvalue.astype(jnp.bfloat16), "ctx", scatter_dimension=1, tiled=True
        ).astype(jnp.float32),
    )
    return (
        grad_q_nope,
        grad_q_rope,
        lat_sum.astype(jnp.bfloat16),
        rope_sum.astype(jnp.bfloat16),
        wkey_share.astype(jnp.bfloat16),
        wvalue_share.astype(jnp.bfloat16),
    )


def solution(mesh):
    placed = (
        P("ctx", "tp", None),
        P("ctx", "tp"),
        P("ctx", None),
        P("ctx", None),
        P("ctx", "tp", None),
        P("tp", None, None),
        P("tp", None, None),
        P(),
    )
    return jax.shard_map(
        per_device,
        mesh=mesh,
        in_specs=placed,
        out_specs=(
            P("ctx", "tp", None),
            P("ctx", "tp"),
            P("ctx", None),
            P("ctx", None),
            P("tp", "ctx", None),
            P("tp", "ctx", None),
        ),
        check_vma=False,
    )
```

profile of v0, /device:TPU:1, one launch (start us, length us, event | category | flops | bytes accessed | tf_op | source)
XLA Modules:
  0.0 406.4 jit_solution(13918449278219055818)
XLA Ops:
  8.1 7.9 %collective-permute-start = (bf16[128,512]{1,0:T(8,128)(2,1)}, bf16[128,512]{1,0:T(8,128)(2,1)}, u32[]{:S(2)}, u32[]{:S(2)}) collective-permute-start(bf16[128,512]{1,0:T(8,128)(2,1)} %param.10), channel_id=1, source_target_pairs={{0,48},{8,56},{16,64},{24,72},{32,80},{40,88},{48,96},{56,104},{64... | collective-permute-start | bytes 393224 | tf_op jit(solution)/shard_map/ppermute | solution.py:15
  16.0 3.5 collective-permute-start.1
  19.5 1.9 collective-permute-start.2
  21.4 4.1 %collective-permute-start.3 = (bf16[128,512]{1,0:T(8,128)(2,1)}, bf16[128,512]{1,0:T(8,128)(2,1)S(1)}, u32[]{:S(2)}, u32[]{:S(2)}) collective-permute-start(bf16[128,512]{1,0:T(8,128)(2,1)} %param.10), channel_id=1, source_target_pairs={{0,24},{8,32},{16,40},{24,48},{32,56},{40,64},{48,72},{56,80},{64,... | collective-permute-start | bytes 393224 | tf_op jit(solution)/shard_map/ppermute | solution.py:15
  25.5 3.7 collective-permute-start.6
  30.7 3.4 convolution_convert_fusion.4
  34.2 2.0 convolution_convert_fusion.3
  36.7 4.6 %collective-permute-start.7 = (bf16[128,64]{0,1:T(8,128)(2,1)S(1)}, bf16[128,64]{0,1:T(8,128)(2,1)S(1)}, u32[]{:S(2)}, u32[]{:S(2)}) collective-permute-start(bf16[128,64]{0,1:T(8,128)(2,1)S(1)} %copy-done.15), channel_id=1, source_target_pairs={{0,40},{8,48},{16,56},{24,64},{32,72},{40,80},{48,88},{56,96},{64,... | collective-permute-start | bytes 49160 | tf_op jit(solution)/shard_map/ppermute | solution.py:15
  42.1 2.9 collective-permute-start.8
  45.8 5.9 %collective-permute-start.9 = (bf16[128,64]{0,1:T(8,128)(2,1)S(1)}, bf16[128,64]{0,1:T(8,128)(2,1)S(1)}, u32[]{:S(2)}, u32[]{:S(2)}) collective-permute-start(bf16[128,64]{0,1:T(8,128)(2,1)S(1)} %copy-done.15), channel_id=1, source_target_pairs={{0,24},{8,32},{16,40},{24,48},{32,56},{40,64},{48,72},{56,80},{64,... | collective-permute-start | bytes 49160 | tf_op jit(solution)/shard_map/ppermute | solution.py:15
  52.5 5.1 %collective-permute-start.10 = (bf16[128,64]{0,1:T(8,128)(2,1)S(1)}, bf16[128,64]{0,1:T(8,128)(2,1)S(1)}, u32[]{:S(2)}, u32[]{:S(2)}) collective-permute-start(bf16[128,64]{0,1:T(8,128)(2,1)S(1)} %copy-done.15), channel_id=1, source_target_pairs={{0,16},{8,24},{16,32},{24,40},{32,48},{40,56},{48,64},{56,72},{64,... | collective-permute-start | bytes 49160 | tf_op jit(solution)/shard_map/ppermute | solution.py:15
  58.5 3.1 collective-permute-start.11
  62.4 5.1 %collective-permute-start.4 = (bf16[128,512]{1,0:T(8,128)(2,1)S(1)}, bf16[128,512]{1,0:T(8,128)(2,1)S(1)}, u32[]{:S(2)}, u32[]{:S(2)}) collective-permute-start(bf16[128,512]{1,0:T(8,128)(2,1)S(1)} %copy-done.14), channel_id=1, source_target_pairs={{0,16},{8,24},{16,32},{24,40},{32,48},{40,56},{48,64},{56,72},{64,... | collective-permute-start | bytes 393224 | tf_op jit(solution)/shard_map/ppermute | solution.py:15
  68.7 4.7 %collective-permute-start.5 = (bf16[128,512]{1,0:T(8,128)(2,1)S(1)}, bf16[128,512]{1,0:T(8,128)(2,1)S(1)}, u32[]{:S(2)}, u32[]{:S(2)}) collective-permute-start(bf16[128,512]{1,0:T(8,128)(2,1)S(1)} %copy-done.14), channel_id=1, source_target_pairs={{0,8},{8,16},{16,24},{24,32},{32,40},{40,48},{48,56},{56,64},{64,7... | collective-permute-start | bytes 393224 | tf_op jit(solution)/shard_map/ppermute | solution.py:15
  76.2 2.3 fusion.40
  79.6 2.2 copy-done.12
  81.7 4.1 %fusion.3 = (f32[128,16]{0,1:T(8,128)S(1)}, bf16[512,16,128]{2,0,1:T(8,128)(2,1)}) fusion(bf16[16,512,128]{2,1,0:T(8,128)(2,1)S(1)} %copy-done.12, f32[16,128,896]{1,2,0:T(8,128)S(1)} %get-tuple-element.43, f32[16,128]{1,0:T(8,128)S(1)} %log_add_fusion, bf16[896,512]{1,0:T(8,128)(2,1)S(1)} %constant_dynamic-update-slice_fusion), kind=kOutput, calls=%fused_computation.8 | convolution fusion | flops 1887959040 | bytes 12468224 | tf_op jit(solution)/shard_map/htk,kl->thl/dot_general | solution.py:78
  85.9 2.5 fusion.1
  88.4 2.4 convolution_convert_fusion
  90.8 1.3 copy-done.5
  92.2 2.1 convert_bitcast_fusion
  94.2 4.6 %copy.92 = bf16[16,128,512]{2,0,1:T(8,128)(2,1)} copy(bf16[16,128,512]{1,2,0:T(8,128)(2,1)} %convert_bitcast_fusion) | data formatting | bytes 4194304 | tf_op jit(solution)/shard_map/convert_element_type | solution.py:141
  99.2 5.9 %fusion.4 = f32[896,512,1]{1,0,2:T(8,128)S(1)} fusion(bf16[16,512,128]{2,1,0:T(8,128)(2,1)} %convolution_convert_fusion.3, f32[16,128,896]{1,2,0:T(8,128)} %copy-done.1, f32[16,128]{1,0:T(8,128)S(1)} %log_add_fusion), kind=kOutput, calls=%fused_computation.9 | convolution fusion | flops 1882718208 | bytes 11280384 | tf_op jit(solution)/shard_map/htk,thl->kl/dot_general | solution.py:105
  105.1 2.1 fusion.41
  107.3 1.9 collective-permute-start.12
  109.2 1.3 collective-permute-start.13
  110.5 1.3 collective-permute-start.14
  111.8 1.3 collective-permute-start.15
  113.1 1.3 collective-permute-start.16
  116.9 3.2 collective-permute-done.14
  120.2 8.0 %collective-permute-done.15 = bf16[128,512]{1,0:T(8,128)(2,1)S(1)} collective-permute-done((bf16[128,512]{1,0:T(8,128)(2,1)S(1)}, bf16[128,512]{1,0:T(8,128)(2,1)S(1)}, u32[]{:S(2)}, u32[]{:S(2)}) %collective-permute-start.15) | collective-permute-done | bytes 131104 | tf_op jit(solution)/shard_map/ppermute | solution.py:15
  128.2 9.6 %collective-permute-done.16 = bf16[128,512]{1,0:T(8,128)(2,1)S(1)} collective-permute-done((bf16[128,512]{1,0:T(8,128)(2,1)S(1)}, bf16[128,512]{1,0:T(8,128)(2,1)S(1)}, u32[]{:S(2)}, u32[]{:S(2)}) %collective-permute-start.16) | collective-permute-done | bytes 131104 | tf_op jit(solution)/shard_map/ppermute | solution.py:15
  137.8 2.2 collective-permute-done.17
  140.8 3.7 convolution_convert_fusion.2
  144.6 3.4 fusion.42
  148.0 4.8 %collective-permute-start.18 = (bf16[128,64]{0,1:T(8,128)(2,1)S(1)}, bf16[128,64]{0,1:T(8,128)(2,1)S(1)}, u32[]{:S(2)}, u32[]{:S(2)}) collective-permute-start(bf16[128,64]{0,1:T(8,128)(2,1)S(1)} %get-tuple-element.36), channel_id=1, source_target_pairs={{8,0},{16,8},{24,16},{32,24},{40,32},{48,40},{56,48},{64,56},{72,6... | collective-permute-start | bytes 49160 | tf_op jit(solution)/shard_map/ppermute | solution.py:15
  153.6 1.3 collective-permute-start.19
  154.9 1.3 collective-permute-start.20
  156.2 1.3 collective-permute-start.21
  162.9 3.7 collective-permute-done.20
  166.6 1.8 collective-permute-done.21
  168.4 3.2 collective-permute-done.22
  171.6 1.4 collective-permute-done.23
  173.0 49.4 %psum.15 = bf16[128,64]{0,1:T(8,128)(2,1)} all-reduce(bf16[128,64]{0,1:T(8,128)(2,1)S(1)} %fusion.37), channel_id=1, replica_groups=mesh['ctx'=32,'tp'=8] {'tp'}, use_global_device_ids=true, to_apply=%region_6.7 | all-reduce | flops 8192 | bytes 32768 | tf_op jit(solution)/shard_map/psum | solution.py:137
  222.4 28.6 %reduce-scatter.3.cloned.1.call-done = bf16[16,4,512]{2,0,1:T(8,128)(2,1)} async-done(((bf16[16,128,512]{2,0,1:T(8,128)(2,1)}), bf16[16,4,512]{2,0,1:T(8,128)(2,1)}) %reduce-scatter.3.cloned.1.call-update) | async-done | bytes 65552 | tf_op jit(solution)/shard_map/reduce_scatter | solution.py:140
  251.0 1.5 copy.96
  252.5 144.9 %reduce-scatter.5.cloned.1.call-done = bf16[16,16,128]{2,1,0:T(8,128)(2,1)} async-done(((bf16[16,512,128]{2,1,0:T(8,128)(2,1)}), bf16[16,16,128]{2,1,0:T(8,128)(2,1)}) %reduce-scatter.5.cloned.1.call-update) | async-done | bytes 65552 | tf_op jit(solution)/shard_map/reduce_scatter | solution.py:143
  397.4 1.6 copy.132
  (88 shorter events, 21.1 us)
Async XLA Ops:
  8.0 22.7 %copy-start = (bf16[16,128,512]{2,1,0:T(8,128)(2,1)S(1)}, bf16[16,128,512]{2,1,0:T(8,128)(2,1)}, u32[]{:S(2)}) copy-start(bf16[16,128,512]{2,1,0:T(8,128)(2,1)} %param.13) | copy-start | bytes 6291460
  8.0 26.1 %copy-start.10 = (bf16[128,16,128]{2,1,0:T(8,128)(2,1)S(1)}, bf16[128,16,128]{2,1,0:T(8,128)(2,1)}, u32[]{:S(2)}) copy-start(bf16[128,16,128]{2,1,0:T(8,128)(2,1)} %param.12) | copy-start | bytes 1572868
  8.0 242.9 %reduce-scatter.3.cloned.1.call-start = ((), (), s32[]{:S(2)}) async-start(), calls=%async_computation.3 | async-start | bytes 2162688 | tf_op jit(solution)/shard_map/reduce_scatter | solution.py:140
  8.1 60.6 %collective-permute-start = (bf16[128,512]{1,0:T(8,128)(2,1)}, bf16[128,512]{1,0:T(8,128)(2,1)}, u32[]{:S(2)}, u32[]{:S(2)}) collective-permute-start(bf16[128,512]{1,0:T(8,128)(2,1)} %param.10), channel_id=1, source_target_pairs={{0,48},{8,56},{16,64},{24,72},{32,80},{40,88},{48,96},{56,104},{64... | collective-permute-start | bytes 393224 | tf_op jit(solution)/shard_map/ppermute | solution.py:15
  16.0 58.3 %collective-permute-start.1 = (bf16[128,512]{1,0:T(8,128)(2,1)}, bf16[128,512]{1,0:T(8,128)(2,1)}, u32[]{:S(2)}, u32[]{:S(2)}) collective-permute-start(bf16[128,512]{1,0:T(8,128)(2,1)} %param.10), channel_id=1, source_target_pairs={{0,40},{8,48},{16,56},{24,64},{32,72},{40,80},{48,88},{56,96},{64,... | collective-permute-start | bytes 393224 | tf_op jit(solution)/shard_map/ppermute | solution.py:15
  19.5 55.7 %collective-permute-start.2 = (bf16[128,512]{1,0:T(8,128)(2,1)}, bf16[128,512]{1,0:T(8,128)(2,1)}, u32[]{:S(2)}, u32[]{:S(2)}) collective-permute-start(bf16[128,512]{1,0:T(8,128)(2,1)} %param.10), channel_id=1, source_target_pairs={{0,32},{8,40},{16,48},{24,56},{32,64},{40,72},{48,80},{56,88},{64,... | collective-permute-start | bytes 393224 | tf_op jit(solution)/shard_map/ppermute | solution.py:15
  21.4 54.7 %collective-permute-start.3 = (bf16[128,512]{1,0:T(8,128)(2,1)}, bf16[128,512]{1,0:T(8,128)(2,1)S(1)}, u32[]{:S(2)}, u32[]{:S(2)}) collective-permute-start(bf16[128,512]{1,0:T(8,128)(2,1)} %param.10), channel_id=1, source_target_pairs={{0,24},{8,32},{16,40},{24,48},{32,56},{40,64},{48,72},{56,80},{64,... | collective-permute-start | bytes 393224 | tf_op jit(solution)/shard_map/ppermute | solution.py:15
  25.5 11.2 %collective-permute-start.6 = (bf16[128,64]{0,1:T(8,128)(2,1)}, bf16[128,64]{0,1:T(8,128)(2,1)S(1)}, u32[]{:S(2)}, u32[]{:S(2)}) collective-permute-start(bf16[128,64]{0,1:T(8,128)(2,1)} %param.11), channel_id=1, source_target_pairs={{0,48},{8,56},{16,64},{24,72},{32,80},{40,88},{48,96},{56,104},{64... | collective-permute-start | bytes 49160 | tf_op jit(solution)/shard_map/ppermute | solution.py:15
  30.7 3.4 copy-start.11
  30.7 5.7 %copy-start.13 = (bf16[128,1024]{1,0:T(8,128)(2,1)S(1)}, bf16[128,1024]{1,0:T(8,128)(2,1)}, u32[]{:S(2)}) copy-start(bf16[128,1024]{1,0:T(8,128)(2,1)} %param.9) | copy-start | bytes 786436
  34.1 2.5 copy-start.15
  34.2 28.2 %copy-start.14 = (bf16[128,512]{1,0:T(8,128)(2,1)S(1)}, bf16[128,512]{1,0:T(8,128)(2,1)}, u32[]{:S(2)}) copy-start(bf16[128,512]{1,0:T(8,128)(2,1)} %param.10) | copy-start | bytes 393220
  36.7 5.4 %collective-permute-start.7 = (bf16[128,64]{0,1:T(8,128)(2,1)S(1)}, bf16[128,64]{0,1:T(8,128)(2,1)S(1)}, u32[]{:S(2)}, u32[]{:S(2)}) collective-permute-start(bf16[128,64]{0,1:T(8,128)(2,1)S(1)} %copy-done.15), channel_id=1, source_target_pairs={{0,40},{8,48},{16,56},{24,64},{32,72},{40,80},{48,88},{56,96},{64,... | collective-permute-start | bytes 49160 | tf_op jit(solution)/shard_map/ppermute | solution.py:15
  42.1 3.7 collective-permute-start.8
  45.8 6.7 %collective-permute-start.9 = (bf16[128,64]{0,1:T(8,128)(2,1)S(1)}, bf16[128,64]{0,1:T(8,128)(2,1)S(1)}, u32[]{:S(2)}, u32[]{:S(2)}) collective-permute-start(bf16[128,64]{0,1:T(8,128)(2,1)S(1)} %copy-done.15), channel_id=1, source_target_pairs={{0,24},{8,32},{16,40},{24,48},{32,56},{40,64},{48,72},{56,80},{64,... | collective-permute-start | bytes 49160 | tf_op jit(solution)/shard_map/ppermute | solution.py:15
  52.5 5.9 %collective-permute-start.10 = (bf16[128,64]{0,1:T(8,128)(2,1)S(1)}, bf16[128,64]{0,1:T(8,128)(2,1)S(1)}, u32[]{:S(2)}, u32[]{:S(2)}) collective-permute-start(bf16[128,64]{0,1:T(8,128)(2,1)S(1)} %copy-done.15), channel_id=1, source_target_pairs={{0,16},{8,24},{16,32},{24,40},{32,48},{40,56},{48,64},{56,72},{64,... | collective-permute-start | bytes 49160 | tf_op jit(solution)/shard_map/ppermute | solution.py:15
  58.5 3.9 collective-permute-start.11
  62.4 13.7 %collective-permute-start.4 = (bf16[128,512]{1,0:T(8,128)(2,1)S(1)}, bf16[128,512]{1,0:T(8,128)(2,1)S(1)}, u32[]{:S(2)}, u32[]{:S(2)}) collective-permute-start(bf16[128,512]{1,0:T(8,128)(2,1)S(1)} %copy-done.14), channel_id=1, source_target_pairs={{0,16},{8,24},{16,32},{24,40},{32,48},{40,56},{48,64},{56,72},{64,... | collective-permute-start | bytes 393224 | tf_op jit(solution)/shard_map/ppermute | solution.py:15
  67.5 8.7 %copy-start.7 = (bf16[16,512,128]{2,1,0:T(8,128)(2,1)S(1)}, bf16[16,512,128]{2,1,0:T(8,128)(2,1)}, u32[]{:S(2)}) copy-start(bf16[16,512,128]{2,1,0:T(8,128)(2,1)} %convolution_convert_fusion.4) | copy-start | bytes 6291460
  68.7 7.5 %collective-permute-start.5 = (bf16[128,512]{1,0:T(8,128)(2,1)S(1)}, bf16[128,512]{1,0:T(8,128)(2,1)S(1)}, u32[]{:S(2)}, u32[]{:S(2)}) collective-permute-start(bf16[128,512]{1,0:T(8,128)(2,1)S(1)} %copy-done.14), channel_id=1, source_target_pairs={{0,8},{8,16},{16,24},{24,32},{32,40},{40,48},{48,56},{56,64},{64,7... | collective-permute-start | bytes 393224 | tf_op jit(solution)/shard_map/ppermute | solution.py:15
  78.6 7.3 %copy-start.1 = (f32[16,128,896]{1,2,0:T(8,128)}, f32[16,128,896]{1,2,0:T(8,128)S(1)}, u32[]{:S(2)}) copy-start(f32[16,128,896]{1,2,0:T(8,128)S(1)} %get-tuple-element.43) | copy-start | bytes 22020100
  78.6 3.2 copy-start.12
  88.4 2.5 copy-start.2
  88.4 3.8 copy-start.9
  90.8 1.3 copy-start.5
  98.9 153.6 %all-reduce.2.cloned.1.call-start = ((), (), s32[]{:S(2)}) async-start(), calls=%async_computation.2 | async-start | bytes 262144 | tf_op jit(solution)/shard_map/psum | solution.py:136
  99.1 6.0 %copy-start.3 = (bf16[16,128,896]{1,2,0:T(8,128)(2,1)S(1)}, bf16[16,128,896]{1,2,0:T(8,128)(2,1)}, u32[]{:S(2)}) copy-start(bf16[16,128,896]{1,2,0:T(8,128)(2,1)} %copy-done.2) | copy-start | bytes 11010052
  99.1 6.0 %copy-start.8 = (bf16[16,512,128]{2,1,0:T(8,128)(2,1)S(1)}, bf16[16,512,128]{2,1,0:T(8,128)(2,1)}, u32[]{:S(2)}) copy-start(bf16[16,512,128]{2,1,0:T(8,128)(2,1)} %convolution_convert_fusion.4) | copy-start | bytes 6291460
  107.3 7.1 %collective-permute-start.12 = (bf16[128,512]{1,0:T(8,128)(2,1)S(1)}, bf16[128,512]{1,0:T(8,128)(2,1)S(1)}, u32[]{:S(2)}, u32[]{:S(2)}) collective-permute-start(bf16[128,512]{1,0:T(8,128)(2,1)S(1)} %get-tuple-element.30), channel_id=1, source_target_pairs={{8,0},{16,8},{24,16},{32,24},{40,32},{48,40},{56,48},{64,56},{72,6... | collective-permute-start | bytes 393224 | tf_op jit(solution)/shard_map/ppermute | solution.py:15
  109.2 7.8 %collective-permute-start.13 = (bf16[128,512]{1,0:T(8,128)(2,1)S(1)}, bf16[128,512]{1,0:T(8,128)(2,1)S(1)}, u32[]{:S(2)}, u32[]{:S(2)}) collective-permute-start(bf16[128,512]{1,0:T(8,128)(2,1)S(1)} %get-tuple-element.35), channel_id=1, source_target_pairs={{16,0},{24,8},{32,16},{40,24},{48,32},{56,40},{64,48},{72,56},{80,... | collective-permute-start | bytes 393224 | tf_op jit(solution)/shard_map/ppermute | solution.py:15
  110.5 9.7 %collective-permute-start.14 = (bf16[128,512]{1,0:T(8,128)(2,1)S(1)}, bf16[128,512]{1,0:T(8,128)(2,1)S(1)}, u32[]{:S(2)}, u32[]{:S(2)}) collective-permute-start(bf16[128,512]{1,0:T(8,128)(2,1)S(1)} %get-tuple-element.34), channel_id=1, source_target_pairs={{24,0},{32,8},{40,16},{48,24},{56,32},{64,40},{72,48},{80,56},{88,... | collective-permute-start | bytes 393224 | tf_op jit(solution)/shard_map/ppermute | solution.py:15
  111.8 16.4 %collective-permute-start.15 = (bf16[128,512]{1,0:T(8,128)(2,1)S(1)}, bf16[128,512]{1,0:T(8,128)(2,1)S(1)}, u32[]{:S(2)}, u32[]{:S(2)}) collective-permute-start(bf16[128,512]{1,0:T(8,128)(2,1)S(1)} %get-tuple-element.33), channel_id=1, source_target_pairs={{32,0},{40,8},{48,16},{56,24},{64,32},{72,40},{80,48},{88,56},{96,... | collective-permute-start | bytes 393224 | tf_op jit(solution)/shard_map/ppermute | solution.py:15
  113.1 24.7 %collective-permute-start.16 = (bf16[128,512]{1,0:T(8,128)(2,1)S(1)}, bf16[128,512]{1,0:T(8,128)(2,1)S(1)}, u32[]{:S(2)}, u32[]{:S(2)}) collective-permute-start(bf16[128,512]{1,0:T(8,128)(2,1)S(1)} %get-tuple-element.32), channel_id=1, source_target_pairs={{40,0},{48,8},{56,16},{64,24},{72,32},{80,40},{88,48},{96,56},{104... | collective-permute-start | bytes 393224 | tf_op jit(solution)/shard_map/ppermute | solution.py:15
  114.4 25.6 %collective-permute-start.17 = (bf16[128,512]{1,0:T(8,128)(2,1)S(1)}, bf16[128,512]{1,0:T(8,128)(2,1)S(1)}, u32[]{:S(2)}, u32[]{:S(2)}) collective-permute-start(bf16[128,512]{1,0:T(8,128)(2,1)S(1)} %get-tuple-element.31), channel_id=1, source_target_pairs={{48,0},{56,8},{64,16},{72,24},{80,32},{88,40},{96,48},{104,56},{11... | collective-permute-start | bytes 393224 | tf_op jit(solution)/shard_map/ppermute | solution.py:15
  140.8 256.6 %reduce-scatter.5.cloned.1.call-start = ((), (), s32[]{:S(2)}) async-start(), calls=%async_computation.4 | async-start | bytes 2162688 | tf_op jit(solution)/shard_map/reduce_scatter | solution.py:143
  144.5 8.3 %copy-start.6 = (bf16[512,16,128]{2,0,1:T(8,128)(2,1)S(1)}, bf16[512,16,128]{2,0,1:T(8,128)(2,1)}, u32[]{:S(2)}) copy-start(bf16[512,16,128]{2,0,1:T(8,128)(2,1)} %copy-done.5) | copy-start | bytes 6291460
  148.0 12.2 %copy-start.4 = (bf16[16,128,896]{1,2,0:T(8,128)(2,1)S(1)}, bf16[16,128,896]{1,2,0:T(8,128)(2,1)}, u32[]{:S(2)}) copy-start(bf16[16,128,896]{1,2,0:T(8,128)(2,1)} %copy-done.2) | copy-start | bytes 11010052
  148.0 10.8 %collective-permute-start.18 = (bf16[128,64]{0,1:T(8,128)(2,1)S(1)}, bf16[128,64]{0,1:T(8,128)(2,1)S(1)}, u32[]{:S(2)}, u32[]{:S(2)}) collective-permute-start(bf16[128,64]{0,1:T(8,128)(2,1)S(1)} %get-tuple-element.36), channel_id=1, source_target_pairs={{8,0},{16,8},{24,16},{32,24},{40,32},{48,40},{56,48},{64,56},{72,6... | collective-permute-start | bytes 49160 | tf_op jit(solution)/shard_map/ppermute | solution.py:15
  153.6 9.3 %collective-permute-start.19 = (bf16[128,64]{0,1:T(8,128)(2,1)S(1)}, bf16[128,64]{0,1:T(8,128)(2,1)S(1)}, u32[]{:S(2)}, u32[]{:S(2)}) collective-permute-start(bf16[128,64]{0,1:T(8,128)(2,1)S(1)} %get-tuple-element.41), channel_id=1, source_target_pairs={{16,0},{24,8},{32,16},{40,24},{48,32},{56,40},{64,48},{72,56},{80,... | collective-permute-start | bytes 49160 | tf_op jit(solution)/shard_map/ppermute | solution.py:15
  154.9 11.7 %collective-permute-start.20 = (bf16[128,64]{0,1:T(8,128)(2,1)S(1)}, bf16[128,64]{0,1:T(8,128)(2,1)S(1)}, u32[]{:S(2)}, u32[]{:S(2)}) collective-permute-start(bf16[128,64]{0,1:T(8,128)(2,1)S(1)} %get-tuple-element.40), channel_id=1, source_target_pairs={{24,0},{32,8},{40,16},{48,24},{56,32},{64,40},{72,48},{80,56},{88,... | collective-permute-start | bytes 49160 | tf_op jit(solution)/shard_map/ppermute | solution.py:15
  156.2 12.1 %collective-permute-start.21 = (bf16[128,64]{0,1:T(8,128)(2,1)S(1)}, bf16[128,64]{0,1:T(8,128)(2,1)S(1)}, u32[]{:S(2)}, u32[]{:S(2)}) collective-permute-start(bf16[128,64]{0,1:T(8,128)(2,1)S(1)} %get-tuple-element.39), channel_id=1, source_target_pairs={{32,0},{40,8},{48,16},{56,24},{64,32},{72,40},{80,48},{88,56},{96,... | collective-permute-start | bytes 49160 | tf_op jit(solution)/shard_map/ppermute | solution.py:15
  157.5 14.0 %collective-permute-start.22 = (bf16[128,64]{0,1:T(8,128)(2,1)S(1)}, bf16[128,64]{0,1:T(8,128)(2,1)S(1)}, u32[]{:S(2)}, u32[]{:S(2)}) collective-permute-start(bf16[128,64]{0,1:T(8,128)(2,1)S(1)} %get-tuple-element.38), channel_id=1, source_target_pairs={{40,0},{48,8},{56,16},{64,24},{72,32},{80,40},{88,48},{96,56},{104... | collective-permute-start | bytes 49160 | tf_op jit(solution)/shard_map/ppermute | solution.py:15
  158.8 14.1 %collective-permute-start.23 = (bf16[128,64]{0,1:T(8,128)(2,1)S(1)}, bf16[128,64]{0,1:T(8,128)(2,1)S(1)}, u32[]{:S(2)}, u32[]{:S(2)}) collective-permute-start(bf16[128,64]{0,1:T(8,128)(2,1)S(1)} %get-tuple-element.37), channel_id=1, source_target_pairs={{48,0},{56,8},{64,16},{72,24},{80,32},{88,40},{96,48},{104,56},{11... | collective-permute-start | bytes 49160 | tf_op jit(solution)/shard_map/ppermute | solution.py:15
Sparse Core Ops, SparseCore 0:
  99.0 151.9 reduce-scatter.2
  254.1 143.3 reduce-scatter.4
Sparse Core Ops, SparseCore 1:
  140.8 107.4 all-reduce.1
where the time goes:
time: 412 us; the launch traced here: 406 us
  waiting for transfers between devices  212 us (51%)
  starting transfers between devices  72.3 us (18%)
  blocking collectives  49.4 us (12%)
  matrix products  36.7 us (9%)
  local copies, waits for them, and re-layouts  16.3 us (4%)
  between operations  16.1 us (4%)
    reduce_scatter x1, waiting for transfers between devices, per_device(): lax.psum_scatter(grad_wvalue.astype(jnp.bfloat16), 'ctx', scatter_dimensi...  145 us
    ppermute x24, starting transfers between devices, passed_along(): return lax.ppermute(block, axis, route)  72 us
    psum x1, blocking collectives, per_device(): lax.psum(rope_total.astype(jnp.bfloat16), 'tp').astype(jnp.float32)  49.4 us
    ppermute x24, waiting for transfers between devices, passed_along(): return lax.ppermute(block, axis, route)  38.5 us
    reduce_scatter x1, waiting for transfers between devices, per_device(): lax.psum_scatter(grad_wkey.astype(jnp.bfloat16), 'ctx', scatter_dimension...  28.6 us
    unnamed x49, local copies, waits for them, and re-layouts  11.6 us
  transfers between devices with their start and end apart: 27, of which 16 were waited for; matrix products, arithmetic and copies ran while one was open for 8% of the time, Pallas kernels for 0%

commit v1 on v0

v1 whole, which is shorter than its diff:
```python
import jax
import jax.numpy as jnp
from jax import lax
from jax.experimental import pallas as pl
from jax.experimental.pallas import tpu as pltpu
from jax.sharding import PartitionSpec as P

NOPE = 128
ROPE = 64
LATENT = 512
WIDE = LATENT + 2 * ROPE
TOK = 128
SPAN = 6
WINDOW = (SPAN + 1) * TOK
HEADS = 16
PACK = 4
GROUPS = HEADS // PACK
COLS = PACK * TOK
SCALE = float(NOPE + ROPE) ** -0.5
MESH = pl.DeviceIdType.MESH
F32 = jnp.float32
BF16 = jnp.bfloat16


def nn(a, b):
    return lax.dot_general(a, b, (((1,), (0,)), ((), ())), preferred_element_type=F32)


def nt(a, b):
    return lax.dot_general(a, b, (((1,), (1,)), ((), ())), preferred_element_type=F32)


def add(*terms):
    total = terms[0].astype(F32)
    for term in terms[1:]:
        total = total + term.astype(F32)
    return total


def iota(shape, dim):
    return lax.broadcasted_iota(jnp.int32, shape, dim)


def kernel(
    lengths,
    q,
    q_rope,
    latent,
    k_rope,
    og,
    wk,
    wv,
    gq,
    gq_rope,
    g_latent,
    g_rope,
    g_wk,
    g_wv,
    kall,
    kw,
    kwt,
    q_all,
    gt_all,
    p_all,
    ds_all,
    s_buf,
    gp_buf,
    bias,
    dk,
    w_out,
    w_r0,
    w_r1,
    w_r2,
    w_v,
    w_rz,
    kg,
    k_r0,
    k_r1,
    k_r2,
    k_sum,
    k_r3,
    k_mid,
    k_r4,
    k_fin,
    k_out,
    own_s,
    own_r,
    ctx_s,
    ctx_r,
    yag_s,
    yag_r,
    sib_s,
    sib_r,
    w0_s,
    w0_r,
    w1_s,
    w1_r,
    w2_s,
    w2_r,
    wz_s,
    wz_r,
    e0_s,
    e0_r,
    e1_s,
    e1_r,
    e2_s,
    e2_r,
    e3_s,
    e3_r,
    e4_s,
    e4_r,
    e5_s,
    e5_r,
):
    me = lax.axis_index("ctx")
    tp = lax.axis_index("tp")
    core = lax.rem(me, 2)
    chip = lax.div(me, 2)
    z = lax.rem(chip, 4)
    x = lax.div(chip, 4)
    y = lax.rem(tp, 4)
    zh = lax.div(tp, 4)
    other = 1 - core

    def place(x_=x, z_=z, core_=core, y_=y, zh_=zh):
        return ((x_ * 4 + z_) * 2 + core_, zh_ * 4 + y_)

    def up(value, step):
        return lax.rem(value + step, 4)

    def chip_at(step):
        return (lax.rem(chip + step + 16, 16) * 2 + core, tp)

    sibling = place(core_=other)
    x_next, x_prev, x_far = up(x, 1), up(x, 3), up(x, 2)
    y_next, y_prev, y_far = up(y, 1), up(y, 3), up(y, 2)

    barrier = pltpu.get_barrier_semaphore()
    peers = [sibling, place(x_=x_next), place(x_=x_prev), place(zh_=1 - zh)]
    for step in (1, 2, 3):
        peers += [place(z_=up(z, step)), chip_at(step), chip_at(-step)]
        peers += [place(y_=up(y, step)), place(y_=up(y, step), core_=other)]
    for peer in peers:
        pl.semaphore_signal(barrier, inc=1, device_id=peer, device_id_type=MESH)

    def remote(src, dst, send, recv, peer):
        return pltpu.make_async_remote_copy(
            src_ref=src,
            dst_ref=dst,
            send_sem=send,
            recv_sem=recv,
            device_id=peer,
            device_id_type=MESH,
        )

    for quarter in range(4):
        rows = slice(quarter * 32, quarter * 32 + 32)
        kall[3, core, quarter, :, :LATENT] = latent[rows, :]
        kall[3, core, quarter, :, LATENT:] = jnp.concatenate([k_rope[rows, :]] * 2, axis=1)
    pl.semaphore_wait(barrier, len(peers))

    own = remote(kall.at[3, core], kall.at[3, core], own_s, own_r, sibling)
    ahead = [
        remote(
            kall.at[3, core, y],
            kall.at[3 - step, core, y],
            ctx_s.at[step - 1],
            ctx_r.at[step - 1],
            chip_at(step),
        )
        for step in (1, 2, 3)
    ]
    for copy in ahead:
        copy.start()
    own.start()

    lane = iota((TOK, 2 * ROPE), 1)

    def project(head, carry):
        rows = pl.ds(pl.multiple_of(head * TOK, TOK), TOK)
        cols = pl.ds(pl.multiple_of(lax.div(head, 2) * 2 * ROPE, 2 * ROPE), 2 * ROPE)
        q_all[rows, :LATENT] = nn(q[head], wk[head]).astype(BF16)
        keep = (lane < ROPE) == (lax.rem(head, 2) == 0)
        q_all[rows, LATENT:] = jnp.where(keep, q_rope[:, cols], jnp.zeros((), BF16))
        gt_all[:, rows] = nt(wv[head], og[head]).astype(BF16)
        return carry

    lax.fori_loop(0, HEADS, project, 0)

    query_pos = me * TOK + iota((1, TOK), 1)
    doc_start = jnp.zeros((1, TOK), jnp.int32)
    begin = jnp.int32(0)
    for doc in range(lengths.shape[0]):
        end = begin + lengths[doc]
        inside = (query_pos >= begin) & (query_pos < end)
        doc_start = doc_start + jnp.where(inside, begin, 0)
        begin = end
    for block in range(SPAN + 1):
        key_pos = (me - SPAN + block) * TOK + iota((TOK, TOK), 0)
        allowed = (key_pos >= doc_start) & (key_pos <= query_pos)
        bias[block * TOK : (block + 1) * TOK, :] = jnp.where(allowed, 0.0, -jnp.inf).astype(F32)

    for copy in ahead:
        copy.wait_recv()
    around = [
        remote(
            kall.at[pl.ds(0, 3), core, y],
            kall.at[pl.ds(0, 3), core, y],
            yag_s.at[step - 1],
            yag_r.at[step - 1],
            place(y_=up(y, step)),
        )
        for step in (1, 2, 3)
    ]
    for copy in around:
        copy.start()
    for copy in around:
        copy.wait_recv()
    across = remote(kall.at[pl.ds(0, 3), core], kall.at[pl.ds(0, 3), core], sib_s, sib_r, sibling)
    across.start()
    own.wait_recv()
    across.wait_recv()

    for block in range(SPAN + 1):
        at = core + block
        keys = kall[lax.div(at, 2), lax.rem(at, 2)].reshape(TOK, WIDE)
        kw[block * TOK : (block + 1) * TOK, :] = keys
        kwt[:, block * TOK : (block + 1) * TOK] = keys.T

    row, col = iota((NOPE, NOPE), 0), iota((NOPE, NOPE), 1)
    owner = ((row >> 4) & 3) * 32 + ((row >> 2) & 3) * 8 + (row >> 6) * 4 + (row & 3)
    by_owner = (col == owner).astype(F32).astype(BF16)
    eye = (col == row).astype(F32).astype(BF16)
    row, col = iota((64, 64), 0), iota((64, 64), 1)
    by_z = (col == ((row >> 2) & 3) * 16 + (row >> 4) * 4 + (row & 3)).astype(F32).astype(BF16)

    def w_stage0(g):
        return remote(w_out.at[g, other], w_r0.at[g], w0_s.at[g], w0_r.at[g], sibling)

    def w_stage1(g):
        return (
            remote(
                w_out.at[g, core, x_far, pl.ds(0, 64)],
                w_r1.at[g, 0],
                w1_s.at[g, 0],
                w1_r.at[g, 0],
                place(x_=x_next),
            ),
            remote(
                w_out.at[g, core, x_far, pl.ds(64, 64)],
                w_r1.at[g, 1],
                w1_s.at[g, 1],
                w1_r.at[g, 1],
                place(x_=x_prev),
            ),
        )

    def w_stage2(g):
        return (
            remote(
                w_out.at[g, core, x_next],
                w_r2.at[g, 0],
                w2_s.at[g, 0],
                w2_r.at[g, 0],
                place(x_=x_next),
            ),
            remote(
                w_out.at[g, core, x_prev],
                w_r2.at[g, 1],
                w2_s.at[g, 1],
                w2_r.at[g, 1],
                place(x_=x_prev),
            ),
        )

    def w_stage3(g):
        return [
            remote(
                w_v.at[g, up(z, step)],
                w_rz.at[g, step - 1],
                wz_s.at[g, step - 1],
                wz_r.at[g, step - 1],
                place(z_=up(z, step)),
            )
            for step in (1, 2, 3)
        ]

    def w_do1(g):
        w_stage0(g).wait_recv()

        def one(part, carry):
            w_out[g, core, part] = add(w_out[g, core, part], w_r0[g, part]).astype(BF16)
            return carry

        lax.fori_loop(0, 4, one, 0)
        for copy in w_stage1(g):
            copy.start()

    def w_do2(g):
        first, second = w_stage1(g)
        first.wait_recv()
        low = w_out[g, core, x_next, 0:64, :]
        w_out[g, core, x_next, 0:64, :] = add(low, w_r1[g, 0]).astype(BF16)
        second.wait_recv()
        high = w_out[g, core, x_prev, 64:128, :]
        w_out[g, core, x_prev, 64:128, :] = add(high, w_r1[g, 1]).astype(BF16)
        for copy in w_stage2(g):
            copy.start()

    def w_do3(g):
        for copy in w_stage2(g):
            copy.wait_recv()
        total = add(w_out[g, core, x], w_r2[g, 0], w_r2[g, 1]).astype(BF16)
        sorted_keys = nn(by_z, total[0:64, :]).astype(BF16)
        for part in range(4):
            w_v[g, part, 0:16, :] = sorted_keys[part * 16 : part * 16 + 16, :]
            for head in range(PACK):
                w_v[g, part, 16:32, head * 128 : head * 128 + 128] = total[
                    64 + head * 16 : 80 + head * 16, part * 128 : part * 128 + 128
                ]
        for copy in w_stage3(g):
            copy.start()

    def w_do4(g):
        for copy in w_stage3(g):
            copy.wait_recv()
        total = add(w_v[g, z], w_rz[g, 0], w_rz[g, 1], w_rz[g, 2]).astype(BF16)
        g_wk[pl.ds(pl.multiple_of(g * 16, 16), 16), :] = total[0:16, :]
        for head in range(PACK):
            g_wv[g * PACK + head] = total[16:32, head * 128 : head * 128 + 128]

    def group(g, carry):
        cols = pl.ds(pl.multiple_of(g * COLS, COLS), COLS)
        s_buf[...] = nt(kw[...], q_all[cols, :])
        high = jnp.full((1, COLS), -jnp.inf, F32)
        for block in range(SPAN + 1):
            rows = slice(block * TOK, (block + 1) * TOK)
            part = s_buf[rows, :] * SCALE + jnp.concatenate([bias[rows, :]] * PACK, axis=1)
            s_buf[rows, :] = part
            high = jnp.maximum(high, jnp.max(part, axis=0, keepdims=True))
        total = jnp.zeros((1, COLS), F32)
        for block in range(SPAN + 1):
            rows = slice(block * TOK, (block + 1) * TOK)
            part = jnp.exp(s_buf[rows, :] - high)
            s_buf[rows, :] = part
            total = total + jnp.sum(part, axis=0, keepdims=True)
        share = 1.0 / total
        for block in range(SPAN + 1):
            rows = slice(block * TOK, (block + 1) * TOK)
            part = s_buf[rows, :] * share
            s_buf[rows, :] = part
            p_all[rows, cols] = part.astype(BF16)

        @pl.when(g > 0)
        def _():
            w_do1(g - 1)

        gp_buf[...] = nn(kw[:, :LATENT], gt_all[:, cols])
        out_t = nn(kwt[:LATENT, :], p_all[:, cols]).astype(BF16)
        correction = jnp.sum(out_t.astype(F32) * gt_all[:, cols].astype(F32), axis=0, keepdims=True)
        for block in range(SPAN + 1):
            rows = slice(block * TOK, (block + 1) * TOK)
            part = SCALE * s_buf[rows, :] * (gp_buf[rows, :] - correction)
            ds_all[rows, cols] = part.astype(BF16)

        @pl.when(g > 0)
        def _():
            w_do2(g - 1)

        dq_t = nn(kwt[...], ds_all[:, cols]).astype(BF16)
        for local in range(PACK):
            head = g * PACK + local
            here = slice(local * TOK, (local + 1) * TOK)
            mine = dq_t[:LATENT, here]
            gq[head] = nt(eye, nn(wk[head], mine).astype(BF16)).astype(BF16)
            turned = nt(by_owner, q[head]).astype(BF16)
            gwk = nt(turned, mine).astype(BF16)
            gwv = nn(out_t[:, here], og[head]).astype(BF16)
            rows = slice(local * 16, local * 16 + 16)
            more = slice(64 + local * 16, 80 + local * 16)
            for half in range(2):
                for part in range(4):
                    begin = half * 64 + part * 16
                    w_out[g, half, part, rows, :] = gwk[begin : begin + 16, :]
                    for depth in range(4):
                        begin = ((part * 4 + depth) * 2 + half) * 16
                        w_out[g, half, part, more, depth * 128 : depth * 128 + 128] = gwv[
                            begin : begin + 16, :
                        ]
        for pair in range(PACK // 2):
            left = dq_t[LATENT : LATENT + ROPE, pair * 256 : pair * 256 + 128]
            right = dq_t[LATENT + ROPE :, pair * 256 + 128 : pair * 256 + 256]
            both = nt(eye, jnp.concatenate([left, right], axis=0)).astype(BF16)
            at = pl.multiple_of((g * 2 + pair) * 128, 128)
            gq_rope[:, pl.ds(at, 128)] = both
        w_stage0(g).start()

        @pl.when(g > 0)
        def _():
            w_do3(g - 1)

        return carry

    lax.fori_loop(0, GROUPS, group, 0)
    last = GROUPS - 1

    dk[...] = nn(ds_all[...], q_all[...])
    w_do1(last)
    dk[:, :LATENT] = dk[:, :LATENT] + nt(p_all[...], gt_all[...])
    for half in range(2):
        for quarter in range(4):
            for block in range(SPAN + 1):
                begin = block * TOK + quarter * 32 + half * 16
                kg[half, quarter, core + block] = dk[begin : begin + 16, :].astype(BF16)
            kg[half, quarter, 7 * other] = jnp.zeros((16, WIDE), BF16)
    e0 = remote(kg.at[other], k_r0, e0_s, e0_r, sibling)
    e0.start()
    w_do2(last)
    e0.wait_recv()
    for quarter in range(4):
        kg[core, quarter] = add(kg[core, quarter], k_r0[quarter]).astype(BF16)
    e1 = (
        remote(
            kg.at[core, y_far, pl.ds(0, 4)], k_r1.at[0], e1_s.at[0], e1_r.at[0], place(y_=y_next)
        ),
        remote(
            kg.at[core, y_far, pl.ds(4, 4)], k_r1.at[1], e1_s.at[1], e1_r.at[1], place(y_=y_prev)
        ),
    )
    for copy in e1:
        copy.start()
    for copy in e1:
        copy.wait_recv()
    low = kg[core, y_next, 0:4]
    kg[core, y_next, 0:4] = add(low, k_r1[0]).astype(BF16)
    high = kg[core, y_prev, 4:8]
    kg[core, y_prev, 4:8] = add(high, k_r1[1]).astype(BF16)
    e2 = (
        remote(kg.at[core, y_next], k_r2.at[0], e2_s.at[0], e2_r.at[0], place(y_=y_next)),
        remote(kg.at[core, y_prev], k_r2.at[1], e2_s.at[1], e2_r.at[1], place(y_=y_prev)),
    )
    for copy in e2:
        copy.start()
    w_do3(last)
    for copy in e2:
        copy.wait_recv()
    k_sum[...] = add(kg[core, y], k_r2[0], k_r2[1]).astype(BF16)
    e3 = [
        remote(
            k_sum.at[pl.ds((3 - step) * 2, 2)],
            k_r3.at[step - 1],
            e3_s.at[step - 1],
            e3_r.at[step - 1],
            chip_at(-step),
        )
        for step in (1, 2, 3)
    ]
    for copy in e3:
        copy.start()
    for g in range(last):
        w_do4(g)
    for copy in e3:
        copy.wait_recv()
    k_mid[...] = add(k_sum[6:8], k_r3[0], k_r3[1], k_r3[2]).astype(BF16)
    e4 = remote(k_mid, k_r4, e4_s, e4_r, place(zh_=1 - zh))
    e4.start()
    w_do4(last)
    e4.wait_recv()
    total = add(k_mid[...], k_r4[...])
    k_fin[:, :, :LATENT] = total[:, :, :LATENT].astype(BF16)
    rope_part = total[:, :, LATENT:].reshape(32, 2 * ROPE)
    rope_part = rope_part + pltpu.roll(rope_part, ROPE, 1)
    k_fin[:, :, LATENT:] = rope_part.reshape(2, 16, 2 * ROPE).astype(BF16)
    k_out[y, core] = k_fin[core]
    e5 = [
        remote(
            k_fin.at[core],
            k_out.at[y, core],
            e5_s.at[step - 1],
            e5_r.at[step - 1],
            place(y_=up(y, step)),
        )
        for step in (1, 2, 3)
    ] + [
        remote(
            k_fin.at[other],
            k_out.at[y, core],
            e5_s.at[3 + step],
            e5_r.at[3 + step],
            place(y_=up(y, step), core_=other),
        )
        for step in (0, 1, 2, 3)
    ]
    for copy in e5:
        copy.start()
    for copy in e5:
        copy.wait_recv()
    for quarter in range(4):
        for half in range(2):
            begin = quarter * 32 + half * 16
            g_latent[begin : begin + 16, :] = k_out[quarter, half, :, :LATENT]
            g_rope[begin : begin + 16, :] = k_out[quarter, half, :, LATENT : LATENT + ROPE]

    own.wait_send()
    across.wait_send()
    e0.wait_send()
    e4.wait_send()
    for copy in [*ahead, *around, *e1, *e2, *e3, *e5]:
        copy.wait_send()
    for g in range(GROUPS):
        for copy in [w_stage0(g), *w_stage1(g), *w_stage2(g), *w_stage3(g)]:
            copy.wait_send()


def per_device(q_nope, q_rope, latent, k_rope, out_grad, w_key, w_value, lengths):
    dma = pltpu.SemaphoreType.DMA
    vmem = pl.BlockSpec(memory_space=pltpu.VMEM)

    def held(*shape, dtype=BF16):
        return pltpu.VMEM(shape, dtype)

    out = pl.pallas_call(
        kernel,
        out_shape=(
            jax.ShapeDtypeStruct((HEADS, TOK, NOPE), BF16),
            jax.ShapeDtypeStruct((TOK, HEADS * ROPE), BF16),
            jax.ShapeDtypeStruct((TOK, LATENT), BF16),
            jax.ShapeDtypeStruct((TOK, ROPE), BF16),
            jax.ShapeDtypeStruct((HEADS * 4, LATENT), BF16),
            jax.ShapeDtypeStruct((HEADS, 16, NOPE), BF16),
        ),
        in_specs=[pl.BlockSpec(memory_space=pltpu.SMEM)] + [vmem] * 7,
        out_specs=[vmem] * 6,
        scratch_shapes=[
            held(4, 2, 4, 32, WIDE),
            held(WINDOW, WIDE),
            held(WIDE, WINDOW),
            held(HEADS * TOK, WIDE),
            held(LATENT, HEADS * TOK),
            held(WINDOW, HEADS * TOK),
            held(WINDOW, HEADS * TOK),
            held(WINDOW, COLS, dtype=F32),
            held(WINDOW, COLS, dtype=F32),
            held(WINDOW, TOK, dtype=F32),
            held(WINDOW, WIDE, dtype=F32),
            held(GROUPS, 2, 4, 128, LATENT),
            held(GROUPS, 4, 128, LATENT),
            held(GROUPS, 2, 64, LATENT),
            held(GROUPS, 2, 128, LATENT),
            held(GROUPS, 4, 32, LATENT),
            held(GROUPS, 3, 32, LATENT),
            held(2, 4, 8, 16, WIDE),
            held(4, 8, 16, WIDE),
            held(2, 4, 16, WIDE),
            held(2, 8, 16, WIDE),
            held(8, 16, WIDE),
            held(3, 2, 16, WIDE),
            held(2, 16, WIDE),
            held(2, 16, WIDE),
            held(2, 16, WIDE),
            held(4, 2, 16, WIDE),
            dma,
            dma,
            dma((3,)),
            dma((3,)),
            dma((3,)),
            dma((3,)),
            dma,
            dma,
            dma((GROUPS,)),
            dma((GROUPS,)),
            dma((GROUPS, 2)),
            dma((GROUPS, 2)),
            dma((GROUPS, 2)),
            dma((GROUPS, 2)),
            dma((GROUPS, 3)),
            dma((GROUPS, 3)),
            dma,
            dma,
            dma((2,)),
            dma((2,)),
            dma((2,)),
            dma((2,)),
            dma((3,)),
            dma((3,)),
            dma,
            dma,
            dma((7,)),
            dma((7,)),
        ],
        compiler_params=pltpu.CompilerParams(
            collective_id=0, has_side_effects=True, vmem_limit_bytes=58 * 2**20
        ),
        cost_estimate=pl.CostEstimate(
            flops=15 * 10**9, bytes_accessed=8 * 10**6, transcendentals=2 * 10**6
        ),
        name="mla_backward",
    )(
        lengths,
        q_nope.transpose(1, 0, 2),
        q_rope,
        latent,
        k_rope,
        out_grad.transpose(1, 0, 2),
        w_key,
        w_value,
    )
    gq, gq_rope, g_latent, g_rope, g_wk, g_wv = out
    return (
        gq.transpose(1, 0, 2),
        gq_rope,
        g_latent,
        g_rope,
        g_wk.reshape(HEADS, 4, LATENT),
        g_wv,
    )


def solution(mesh):
    placed = (
        P("ctx", "tp", None),
        P("ctx", "tp"),
        P("ctx", None),
        P("ctx", None),
        P("ctx", "tp", None),
        P("tp", None, None),
        P("tp", None, None),
        P(),
    )
    return jax.shard_map(
        per_device,
        mesh=mesh,
        in_specs=placed,
        out_specs=(
            P("ctx", "tp", None),
            P("ctx", "tp"),
            P("ctx", None),
            P("ctx", None),
            P("tp", "ctx", None),
            P("tp", "ctx", None),
        ),
        check_vma=False,
    )
```

time: 412 us -> 114 us (0.28); the launches traced: 406 us -> 114 us
  waiting for transfers between devices: 212 us -> 0 us
  Pallas kernels: 0 us -> 99.4 us
  starting transfers between devices: 72.3 us -> 0 us
  blocking collectives: 49.4 us -> 0 us
  matrix products: 36.7 us -> 0 us
  between operations: 16.1 us -> 0.64 us
    reduce_scatter x2 -> x0, waiting for transfers between devices: 173 us -> none  [the longest x1 145 us: per_device(): lax.psum_scatter(grad_wvalue.astype(jnp.bfloat16), 'ctx', scatter_dimensi...]
    pallas_call x0 -> x1, Pallas kernels: none -> 99.4 us  [per_device(): pl.pallas_call(kernel, out_shape=(jax.ShapeDtypeStruct((HEADS, TOK, NOPE)...]
    ppermute x24 -> x0, starting transfers between devices: 72 us -> none  [passed_along(): return lax.ppermute(block, axis, route)]
    psum x1 -> x0, blocking collectives: 49.4 us -> none  [per_device(): lax.psum(rope_total.astype(jnp.bfloat16), 'tp').astype(jnp.float32)]
    ppermute x24 -> x0, waiting for transfers between devices: 38.5 us -> none  [passed_along(): return lax.ppermute(block, axis, route)]
    dot_general x14 -> x0, matrix products: 36.7 us -> none  [the longest x1 5.93 us: backward_terms(): jnp.einsum('htk,thl->kl', prob16, grad_lat_out, preferred_element_type=jn...]
    convert_element_type x1 -> x0, local copies, waits for them, and re-layouts: 4.6 us -> none  [per_device(): grad_wkey.astype(jnp.bfloat16)]
    unnamed x49 -> x6, local copies, waits for them, and re-layouts: 11.6 us -> 9.77 us
  transfers between devices with their start and end apart: 27 -> 0, of which waited for: 16 -> 0; matrix products, arithmetic and copies ran while one was open for 8% -> 0% of each run, Pallas kernels for 0% -> 0%
where the time goes in v1:
time: 114 us
  Pallas kernels  99.4 us (87%)
  local copies, waits for them, and re-layouts  13.7 us (12%)
    pallas_call x1, Pallas kernels, per_device(): pl.pallas_call(kernel, out_shape=(jax.ShapeDtypeStruct((HEADS, TOK, NOPE)...  99.4 us
    unnamed x6, local copies, waits for them, and re-layouts  9.77 us
    transpose x1, local copies, waits for them, and re-layouts, per_device(): out_grad.transpose(1, 0, 2)  2.42 us

profile of v1, /device:TPU:1, one launch (start us, length us, event | category | flops | bytes accessed | tf_op | source)
XLA Modules:
  0.0 113.7 jit_solution(10042193513568916126)
XLA Ops:
  0.6 1.4 %copy.16.k_rope = bf16[128,64]{1,0:T(8,128)(2,1)} copy(bf16[128,64]{0,1:T(8,128)(2,1)} %param.11) | data formatting | bytes 32768 | tf_op args[3]
  2.1 2.4 %copy_bitcast_fusion = (bf16[16,128,128]{2,1,0:T(8,128)(2,1)}, bf16[16,128,128]{2,1,0:T(8,128)(2,1)}) fusion(bf16[128,16,128]{2,1,0:T(8,128)(2,1)} %param.12, bf16[128,16,128]{2,1,0:T(8,128)(2,1)} %param.8), kind=kLoop, calls=%fused_computation | loop fusion | bytes 2097152 | tf_op jit(solution)/shard_map/transpose | solution.py:604
  4.5 99.4 %mla_backward.1 = (bf16[16,128,128]{2,1,0:T(8,128)(2,1)}, bf16[128,1024]{1,0:T(8,128)(2,1)}, bf16[128,512]{1,0:T(8,128)(2,1)}, bf16[128,64]{1,0:T(8,128)(2,1)}, ...) custom-call(s32[6]{0:T(128)} %lengths.1, bf16[16,128,128]{2,1,0:T(8,128)(2,1)} %get-tuple-element.25.q, ...), custom_call_target="tpu_custom_call" | custom-call | flops 15000000512 | bytes 8000000 | tf_op jit(solution)/shard_map/mla_backward/pallas_call | solution.py:522
  103.9 2.2 %copy.17 = bf16[128,16,128]{2,1,0:T(8,128)(2,1)} copy(bf16[128,16,128]{2,0,1:T(8,128)(2,1)} %bitcast.5) | data formatting | bytes 1048576
  106.0 1.4 %copy.18 = bf16[128,64]{0,1:T(8,128)(2,1)} copy(bf16[128,64]{1,0:T(8,128)(2,1)} %get-tuple-element.21) | data formatting | bytes 32768
  107.5 1.5 %reshape.15 = bf16[16,4,512]{2,1,0:T(4,128)(2,1)} reshape(bf16[64,512]{1,0:T(8,128)(2,1)} %get-tuple-element.16) | data formatting | bytes 131072 | tf_op jit(solution)/shard_map/reshape | solution.py:614
  109.0 1.7 %copy.24 = bf16[128,1024]{1,0:T(8,128)(2,1)} copy(bf16[128,1024]{1,0:T(8,128)(2,1)} %get-tuple-element.33) | data formatting | bytes 524288
  110.6 1.6 %copy.25 = bf16[128,512]{1,0:T(8,128)(2,1)} copy(bf16[128,512]{1,0:T(8,128)(2,1)} %get-tuple-element.34) | data formatting | bytes 262144
  112.2 1.5 %copy.26 = bf16[16,16,128]{2,1,0:T(8,128)(2,1)} copy(bf16[16,16,128]{2,1,0:T(8,128)(2,1)} %get-tuple-element.37) | data formatting | bytes 131072

commit v2 on v1

v2 whole, which is shorter than its diff:
```python
import jax
import jax.numpy as jnp
from jax import lax
from jax.experimental import pallas as pl
from jax.experimental.pallas import tpu as pltpu
from jax.sharding import PartitionSpec as P

NOPE = 128
ROPE = 64
LATENT = 512
WIDE = LATENT + 2 * ROPE
TOK = 128
SPAN = 6
WINDOW = (SPAN + 1) * TOK
HEADS = 16
PACK = 4
GROUPS = HEADS // PACK
JOBS = 2 * GROUPS
COLS = PACK * TOK
SCALE = float(NOPE + ROPE) ** -0.5
MESH = pl.DeviceIdType.MESH
F32 = jnp.float32
BF16 = jnp.bfloat16


def nn(a, b):
    return lax.dot_general(a, b, (((1,), (0,)), ((), ())), preferred_element_type=F32)


def nt(a, b):
    return lax.dot_general(a, b, (((1,), (1,)), ((), ())), preferred_element_type=F32)


def add(*terms):
    total = terms[0].astype(F32)
    for term in terms[1:]:
        total = total + term.astype(F32)
    return total


def iota(shape, dim):
    return lax.broadcasted_iota(jnp.int32, shape, dim)


def kernel(
    lengths,
    q_hbm,
    qr_hbm,
    latent,
    rope_t,
    og_hbm,
    wk_hbm,
    wv_hbm,
    gq,
    gq_rope,
    g_latent,
    g_rope_t,
    g_wk,
    g_wv,
    q_in,
    og_in,
    q_rope,
    wk,
    wv,
    og,
    qt,
    gq_t,
    kall,
    kw,
    kwt,
    q_all,
    gt_all,
    p_all,
    ds_all,
    s_buf,
    gp_buf,
    bias,
    w_out,
    w_r0,
    w_r1,
    w_r2,
    w_v,
    w_rz,
    kg,
    k_r0,
    k_r1,
    k_r2,
    k_sum,
    k_r3,
    k_mid,
    k_r4,
    k_fin,
    k_out,
    load_s,
    own_s,
    own_r,
    ctx_s,
    ctx_r,
    yag_s,
    yag_r,
    sib_s,
    sib_r,
    w0_s,
    w0_r,
    w1_s,
    w1_r,
    w2_s,
    w2_r,
    wz_s,
    wz_r,
    e0_s,
    e0_r,
    e1_s,
    e1_r,
    e2_s,
    e2_r,
    e3_s,
    e3_r,
    e4_s,
    e4_r,
    e5_s,
    e5_r,
):
    me = lax.axis_index("ctx")
    tp = lax.axis_index("tp")
    core = lax.rem(me, 2)
    chip = lax.div(me, 2)
    z = lax.rem(chip, 4)
    x = lax.div(chip, 4)
    y = lax.rem(tp, 4)
    zh = lax.div(tp, 4)
    other = 1 - core

    def place(x_=x, z_=z, core_=core, y_=y, zh_=zh):
        return ((x_ * 4 + z_) * 2 + core_, zh_ * 4 + y_)

    def up(value, step):
        return lax.rem(value + step, 4)

    def chip_at(step):
        return (lax.rem(chip + step + 16, 16) * 2 + core, tp)

    sibling = place(core_=other)
    x_next, x_prev, x_far = up(x, 1), up(x, 3), up(x, 2)
    y_next, y_prev, y_far = up(y, 1), up(y, 3), up(y, 2)

    barrier = pltpu.get_barrier_semaphore()
    peers = [sibling, place(x_=x_next), place(x_=x_prev), place(zh_=1 - zh)]
    for step in (1, 2, 3):
        peers += [place(z_=up(z, step)), chip_at(step), chip_at(-step)]
        peers += [place(y_=up(y, step)), place(y_=up(y, step), core_=other)]
    for peer in peers:
        pl.semaphore_signal(barrier, inc=1, device_id=peer, device_id_type=MESH)

    loads = [
        pltpu.make_async_copy(src, dst, load_s.at[n])
        for n, (src, dst) in enumerate(
            [(q_hbm, q_in), (wk_hbm, wk), (og_hbm, og_in), (wv_hbm, wv), (qr_hbm, q_rope)]
        )
    ]
    for copy in loads:
        copy.start()

    def remote(src, dst, send, recv, peer):
        return pltpu.make_async_remote_copy(
            src_ref=src,
            dst_ref=dst,
            send_sem=send,
            recv_sem=recv,
            device_id=peer,
            device_id_type=MESH,
        )

    rope = rope_t[...].T
    rope = jnp.concatenate([rope, rope], axis=1)
    for quarter in range(4):
        rows = slice(quarter * 32, quarter * 32 + 32)
        kall[3, core, quarter, :, :LATENT] = latent[rows, :]
        kall[3, core, quarter, :, LATENT:] = rope[rows, :]
    pl.semaphore_wait(barrier, len(peers))

    own = remote(kall.at[3, core], kall.at[3, core], own_s, own_r, sibling)
    ahead = [
        remote(
            kall.at[3, core, y],
            kall.at[3 - step, core, y],
            ctx_s.at[step - 1],
            ctx_r.at[step - 1],
            chip_at(step),
        )
        for step in (1, 2, 3)
    ]
    for copy in ahead:
        copy.start()
    own.start()

    row, col = iota((NOPE, NOPE), 0), iota((NOPE, NOPE), 1)
    owner = ((row >> 4) & 3) * 32 + ((row >> 2) & 3) * 8 + (row >> 6) * 4 + (row & 3)
    by_owner = (col == owner).astype(F32).astype(BF16)
    eye = (col == row).astype(F32).astype(BF16)
    row, col = iota((64, 64), 0), iota((64, 64), 1)
    by_z = (col == ((row >> 2) & 3) * 16 + (row >> 4) * 4 + (row & 3)).astype(F32).astype(BF16)

    lane = iota((TOK, 2 * ROPE), 1)

    def project(head, carry):
        rows = pl.ds(pl.multiple_of(head * TOK, TOK), TOK)
        cols = pl.ds(pl.multiple_of(lax.div(head, 2) * 2 * ROPE, 2 * ROPE), 2 * ROPE)
        mine = gq_t[head]
        q_all[rows, :LATENT] = nn(mine, wk[head]).astype(BF16)
        keep = (lane < ROPE) == (lax.rem(head, 2) == 0)
        q_all[rows, LATENT:] = jnp.where(keep, q_rope[:, cols], jnp.zeros((), BF16))
        qt[head] = nt(by_owner, mine).astype(BF16)
        gt_all[:, rows] = nt(wv[head], og[head]).astype(BF16)
        return carry

    for copy in loads:
        copy.wait()
    gq_t[...] = jnp.swapaxes(q_in[...], 0, 1)
    og[...] = jnp.swapaxes(og_in[...], 0, 1)
    lax.fori_loop(0, HEADS // 2, project, 0)

    around = []
    for near in (1, 2, 3):
        ahead[near - 1].wait_recv()
        part = kall.at[3 - near, core, y]
        around.append(
            [
                remote(
                    part,
                    part,
                    yag_s.at[near - 1, step - 1],
                    yag_r.at[near - 1, step - 1],
                    place(y_=up(y, step)),
                )
                for step in (1, 2, 3)
            ]
        )
        for copy in around[-1]:
            copy.start()

    lax.fori_loop(HEADS // 2, HEADS, project, 0)

    query_pos = me * TOK + iota((1, TOK), 1)
    doc_start = jnp.zeros((1, TOK), jnp.int32)
    begin = jnp.int32(0)
    for doc in range(lengths.shape[0]):
        end = begin + lengths[doc]
        inside = (query_pos >= begin) & (query_pos < end)
        doc_start = doc_start + jnp.where(inside, begin, 0)
        begin = end
    for block in range(SPAN + 1):
        key_pos = (me - SPAN + block) * TOK + iota((TOK, TOK), 0)
        allowed = (key_pos >= doc_start) & (key_pos <= query_pos)
        bias[block * TOK : (block + 1) * TOK, :] = jnp.where(allowed, 0.0, -jnp.inf).astype(F32)

    across = []
    for near in (1, 2, 3):
        for copy in around[near - 1]:
            copy.wait_recv()
        part = kall.at[3 - near, core]
        across.append(remote(part, part, sib_s.at[near - 1], sib_r.at[near - 1], sibling))
        across[-1].start()
    own.wait_recv()
    for copy in across:
        copy.wait_recv()

    for block in range(SPAN + 1):
        at = core + block
        keys = kall[lax.div(at, 2), lax.rem(at, 2)].reshape(TOK, WIDE)
        kw[block * TOK : (block + 1) * TOK, :] = keys
        kwt[:, block * TOK : (block + 1) * TOK] = keys.T

    def w_stage0(g):
        return remote(w_out.at[g, other], w_r0.at[g], w0_s.at[g], w0_r.at[g], sibling)

    def w_stage1(g):
        return (
            remote(
                w_out.at[g, core, x_far, pl.ds(0, 32)],
                w_r1.at[g, 0],
                w1_s.at[g, 0],
                w1_r.at[g, 0],
                place(x_=x_next),
            ),
            remote(
                w_out.at[g, core, x_far, pl.ds(32, 32)],
                w_r1.at[g, 1],
                w1_s.at[g, 1],
                w1_r.at[g, 1],
                place(x_=x_prev),
            ),
        )

    def w_stage2(g):
        return (
            remote(
                w_out.at[g, core, x_next],
                w_r2.at[g, 0],
                w2_s.at[g, 0],
                w2_r.at[g, 0],
                place(x_=x_next),
            ),
            remote(
                w_out.at[g, core, x_prev],
                w_r2.at[g, 1],
                w2_s.at[g, 1],
                w2_r.at[g, 1],
                place(x_=x_prev),
            ),
        )

    def w_stage3(g):
        return [
            remote(
                w_v.at[g, up(z, step)],
                w_rz.at[g, step - 1],
                wz_s.at[g, step - 1],
                wz_r.at[g, step - 1],
                place(z_=up(z, step)),
            )
            for step in (1, 2, 3)
        ]

    def w_do1(g):
        w_stage0(g).wait_recv()

        def one(part, carry):
            w_out[g, core, part] = add(w_out[g, core, part], w_r0[g, part]).astype(BF16)
            return carry

        lax.fori_loop(0, 4, one, 0)
        for copy in w_stage1(g):
            copy.start()

    def w_do2(g):
        first, second = w_stage1(g)
        first.wait_recv()
        low = w_out[g, core, x_next, 0:32, :]
        w_out[g, core, x_next, 0:32, :] = add(low, w_r1[g, 0]).astype(BF16)
        second.wait_recv()
        high = w_out[g, core, x_prev, 32:64, :]
        w_out[g, core, x_prev, 32:64, :] = add(high, w_r1[g, 1]).astype(BF16)
        for copy in w_stage2(g):
            copy.start()

    def w_do3(g, of_key):
        for copy in w_stage2(g):
            copy.wait_recv()
        total = add(w_out[g, core, x], w_r2[g, 0], w_r2[g, 1]).astype(BF16)
        if of_key:
            total = nn(by_z, total).astype(BF16)
            for part in range(4):
                w_v[g, part] = total[part * 16 : part * 16 + 16, :]
        else:
            for part in range(4):
                for head in range(PACK):
                    w_v[g, part, :, head * 128 : head * 128 + 128] = total[
                        head * 16 : head * 16 + 16, part * 128 : part * 128 + 128
                    ]
        for copy in w_stage3(g):
            copy.start()

    def w_do4(g, of_key):
        for copy in w_stage3(g):
            copy.wait_recv()
        total = add(w_v[g, z], w_rz[g, 0], w_rz[g, 1], w_rz[g, 2]).astype(BF16)
        for local in range(PACK):
            if of_key:
                g_wk[(g - GROUPS) * PACK + local] = total[local * 4 : local * 4 + 4, :]
            else:
                g_wv[g * PACK + local] = total[:, local * 128 : local * 128 + 128]

    def group(g, carry):
        cols = pl.ds(pl.multiple_of(g * COLS, COLS), COLS)
        s_buf[...] = nt(kw[...], q_all[cols, :])
        @pl.when(g > 0)
        def _():
            w_do1(g - 1)

        high = jnp.full((1, COLS), -jnp.inf, F32)
        for block in range(SPAN + 1):
            rows = slice(block * TOK, (block + 1) * TOK)
            part = s_buf[rows, :] * SCALE + jnp.concatenate([bias[rows, :]] * PACK, axis=1)
            s_buf[rows, :] = part
            high = jnp.maximum(high, jnp.max(part, axis=0, keepdims=True))
        total = jnp.zeros((1, COLS), F32)
        for block in range(SPAN + 1):
            rows = slice(block * TOK, (block + 1) * TOK)
            part = jnp.exp(s_buf[rows, :] - high)
            s_buf[rows, :] = part
            total = total + jnp.sum(part, axis=0, keepdims=True)
        share = 1.0 / total
        for block in range(SPAN + 1):
            rows = slice(block * TOK, (block + 1) * TOK)
            part = s_buf[rows, :] * share
            s_buf[rows, :] = part
            p_all[rows, cols] = part.astype(BF16)

        @pl.when(g > 0)
        def _():
            w_do2(g - 1)

        gp_buf[...] = nn(kw[:, :LATENT], gt_all[:, cols])
        out_t = nn(kwt[:LATENT, :], p_all[:, cols]).astype(BF16)
        correction = jnp.sum(out_t.astype(F32) * gt_all[:, cols].astype(F32), axis=0, keepdims=True)
        for block in range(SPAN + 1):
            rows = slice(block * TOK, (block + 1) * TOK)
            part = SCALE * s_buf[rows, :] * (gp_buf[rows, :] - correction)
            ds_all[rows, cols] = part.astype(BF16)

        for local in range(PACK):
            gwv = nn(out_t[:, local * TOK : (local + 1) * TOK], og[g * PACK + local]).astype(BF16)
            rows = slice(local * 16, local * 16 + 16)
            for half in range(2):
                for part in range(4):
                    for depth in range(4):
                        begin = ((part * 4 + depth) * 2 + half) * 16
                        w_out[g, half, part, rows, depth * 128 : depth * 128 + 128] = gwv[
                            begin : begin + 16, :
                        ]
        w_stage0(g).start()

        @pl.when(g > 0)
        def _():
            w_do3(g - 1, False)

        return carry

    def second(g):
        cols = slice(g * COLS, (g + 1) * COLS)
        dq_t = nn(kwt[...], ds_all[:, cols]).astype(BF16)
        for local in range(PACK):
            head = g * PACK + local
            here = slice(local * TOK, (local + 1) * TOK)
            mine = dq_t[:LATENT, here]
            gq_t[head] = nt(eye, nn(wk[head], mine).astype(BF16)).astype(BF16)
            gwk = nt(qt[head], mine).astype(BF16)
            rows = slice(local * 16, local * 16 + 16)
            for half in range(2):
                for part in range(4):
                    begin = half * 64 + part * 16
                    w_out[GROUPS + g, half, part, rows, :] = gwk[begin : begin + 16, :]
        for pair in range(PACK // 2):
            left = dq_t[LATENT : LATENT + ROPE, pair * 256 : pair * 256 + 128]
            right = dq_t[LATENT + ROPE :, pair * 256 + 128 : pair * 256 + 256]
            both = nt(eye, jnp.concatenate([left, right], axis=0)).astype(BF16)
            gq_rope[:, (g * 2 + pair) * 128 : (g * 2 + pair + 1) * 128] = both
        w_stage0(GROUPS + g).start()

    lax.fori_loop(0, GROUPS, group, 0)
    last = GROUPS - 1

    def key_terms(first, after):
        rows = slice(first * TOK, after * TOK)
        wide = nn(ds_all[rows, :], q_all[...])
        narrow = wide[:, :LATENT] + nt(p_all[rows, :], gt_all[...])
        narrow, side = narrow.astype(BF16), wide[:, LATENT:].astype(BF16)
        for block in range(first, after):
            for quarter in range(4):
                for half in range(2):
                    begin = (block - first) * TOK + quarter * 32 + half * 16
                    kg[half, quarter, core + block, :, :LATENT] = narrow[begin : begin + 16, :]
                    kg[half, quarter, core + block, :, LATENT:] = side[begin : begin + 16, :]

    def e0(n):
        blocks = pl.ds(4 * n, 4)
        return remote(
            kg.at[other, :, blocks], k_r0.at[:, blocks], e0_s.at[n], e0_r.at[n], sibling
        )

    def e1(n):
        return [
            remote(
                kg.at[core, y_far, pl.ds(4 * n + 2 * way, 2)],
                k_r1.at[n, way],
                e1_s.at[n, way],
                e1_r.at[n, way],
                place(y_=y_to),
            )
            for way, y_to in ((0, y_next), (1, y_prev))
        ]

    def e2(n):
        return [
            remote(
                kg.at[core, y_to, pl.ds(4 * n, 4)],
                k_r2.at[n, way],
                e2_s.at[n, way],
                e2_r.at[n, way],
                place(y_=y_to),
            )
            for way, y_to in ((0, y_next), (1, y_prev))
        ]

    def e3(step):
        return remote(
            k_sum.at[pl.ds((3 - step) * 2, 2)],
            k_r3.at[step - 1],
            e3_s.at[step - 1],
            e3_r.at[step - 1],
            chip_at(-step),
        )

    def k_do1(n):
        e0(n).wait_recv()
        blocks = slice(4 * n, 4 * n + 4)
        for quarter in range(4):
            kg[core, quarter, blocks] = add(kg[core, quarter, blocks], k_r0[quarter, blocks]).astype(
                BF16
            )
        for copy in e1(n):
            copy.start()

    def k_do2(n):
        for way, (copy, y_to) in enumerate(zip(e1(n), (y_next, y_prev))):
            copy.wait_recv()
            blocks = slice(4 * n + 2 * way, 4 * n + 2 * way + 2)
            kg[core, y_to, blocks] = add(kg[core, y_to, blocks], k_r1[n, way]).astype(BF16)
        for copy in e2(n):
            copy.start()

    def k_do3(n):
        for copy in e2(n):
            copy.wait_recv()
        blocks = slice(4 * n, 4 * n + 4)
        k_sum[blocks] = add(kg[core, y, blocks], k_r2[n, 0], k_r2[n, 1]).astype(BF16)
        for step in ((3, 2), (1,))[n]:
            e3(step).start()

    for half in range(2):
        for quarter in range(4):
            kg[half, quarter, 7 * other] = jnp.zeros((16, WIDE), BF16)
    w_do1(last)
    key_terms(0, 4)
    e0(0).start()
    w_do2(last)
    key_terms(4, 7)
    e0(1).start()
    k_do1(0)
    second(0)
    k_do1(1)
    w_do3(last, False)
    k_do2(0)
    second(1)
    k_do2(1)
    k_do3(0)
    w_do1(GROUPS)
    second(2)
    k_do3(1)
    w_do2(GROUPS)
    w_do1(GROUPS + 1)
    second(3)
    for step in (1, 2, 3):
        e3(step).wait_recv()
    k_mid[...] = add(k_sum[6:8], k_r3[0], k_r3[1], k_r3[2]).astype(BF16)
    e4 = remote(k_mid, k_r4, e4_s, e4_r, place(zh_=1 - zh))
    e4.start()
    w_do3(GROUPS, True)
    w_do2(GROUPS + 1)
    w_do1(GROUPS + 2)
    w_do1(GROUPS + 3)
    gq[...] = jnp.swapaxes(gq_t[...], 0, 1)
    e4.wait_recv()
    total = add(k_mid[...], k_r4[...])
    k_fin[:, :, :LATENT] = total[:, :, :LATENT].astype(BF16)
    rope_part = total[:, :, LATENT:].reshape(32, 2 * ROPE)
    rope_part = rope_part + pltpu.roll(rope_part, ROPE, 1)
    k_fin[:, :, LATENT:] = rope_part.reshape(2, 16, 2 * ROPE).astype(BF16)
    k_out[y, core] = k_fin[core]
    e5 = [
        remote(
            k_fin.at[core],
            k_out.at[y, core],
            e5_s.at[step - 1],
            e5_r.at[step - 1],
            place(y_=up(y, step)),
        )
        for step in (1, 2, 3)
    ] + [
        remote(
            k_fin.at[other],
            k_out.at[y, core],
            e5_s.at[3 + step],
            e5_r.at[3 + step],
            place(y_=up(y, step), core_=other),
        )
        for step in (0, 1, 2, 3)
    ]
    for copy in e5:
        copy.start()
    w_do3(GROUPS + 1, True)
    w_do2(GROUPS + 2)
    w_do2(GROUPS + 3)
    for g in range(GROUPS):
        w_do4(g, False)
    w_do3(GROUPS + 2, True)
    w_do3(GROUPS + 3, True)
    for copy in e5:
        copy.wait_recv()
    for quarter in range(4):
        for half in range(2):
            begin = quarter * 32 + half * 16
            g_latent[begin : begin + 16, :] = k_out[quarter, half, :, :LATENT]
    g_rope_t[...] = k_out[:, :, :, LATENT:].reshape(TOK, 2 * ROPE).T[:ROPE, :]
    for g in range(GROUPS, JOBS):
        w_do4(g, True)

    own.wait_send()
    e4.wait_send()
    for n in range(2):
        for copy in [e0(n), *e1(n), *e2(n)]:
            copy.wait_send()
    for copy in [*ahead, *across, *e5, *(copy for three in around for copy in three)]:
        copy.wait_send()
    for step in (1, 2, 3):
        e3(step).wait_send()
    for g in range(JOBS):
        for copy in [w_stage0(g), *w_stage1(g), *w_stage2(g), *w_stage3(g)]:
            copy.wait_send()


def hand_over(*refs):
    count = len(refs) // 2
    for source, target in zip(refs[:count], refs[count:]):
        target[...] = source[...]


def per_device(q_nope, q_rope, latent, k_rope, out_grad, w_key, w_value, lengths):
    dma = pltpu.SemaphoreType.DMA
    vmem = pl.BlockSpec(memory_space=pltpu.VMEM)
    hbm = pl.BlockSpec(memory_space=pl.ANY)

    def held(*shape, dtype=BF16):
        return pltpu.VMEM(shape, dtype)

    out = pl.pallas_call(
        kernel,
        out_shape=(
            jax.ShapeDtypeStruct((TOK, HEADS, NOPE), BF16),
            jax.ShapeDtypeStruct((TOK, HEADS * ROPE), BF16),
            jax.ShapeDtypeStruct((TOK, LATENT), BF16),
            jax.ShapeDtypeStruct((ROPE, TOK), BF16),
            jax.ShapeDtypeStruct((HEADS, 4, LATENT), BF16),
            jax.ShapeDtypeStruct((HEADS, 16, NOPE), BF16),
        ),
        in_specs=[pl.BlockSpec(memory_space=pltpu.SMEM), hbm, hbm, vmem, vmem, hbm, hbm, hbm],
        out_specs=[vmem] * 6,
        scratch_shapes=[
            held(TOK, HEADS, NOPE),
            held(TOK, HEADS, NOPE),
            held(TOK, HEADS * ROPE),
            held(HEADS, NOPE, LATENT),
            held(HEADS, LATENT, NOPE),
            held(HEADS, TOK, NOPE),
            held(HEADS, NOPE, TOK),
            held(HEADS, TOK, NOPE),
            held(4, 2, 4, 32, WIDE),
            held(WINDOW, WIDE),
            held(WIDE, WINDOW),
            held(HEADS * TOK, WIDE),
            held(LATENT, HEADS * TOK),
            held(WINDOW, HEADS * TOK),
            held(WINDOW, HEADS * TOK),
            held(WINDOW, COLS, dtype=F32),
            held(WINDOW, COLS, dtype=F32),
            held(WINDOW, TOK, dtype=F32),
            held(JOBS, 2, 4, 64, LATENT),
            held(JOBS, 4, 64, LATENT),
            held(JOBS, 2, 32, LATENT),
            held(JOBS, 2, 64, LATENT),
            held(JOBS, 4, 16, LATENT),
            held(JOBS, 3, 16, LATENT),
            held(2, 4, 8, 16, WIDE),
            held(4, 8, 16, WIDE),
            held(2, 2, 2, 16, WIDE),
            held(2, 2, 4, 16, WIDE),
            held(8, 16, WIDE),
            held(3, 2, 16, WIDE),
            held(2, 16, WIDE),
            held(2, 16, WIDE),
            held(2, 16, WIDE),
            held(4, 2, 16, WIDE),
            dma((5,)),
            dma,
            dma,
            dma((3,)),
            dma((3,)),
            dma((3, 3)),
            dma((3, 3)),
            dma((3,)),
            dma((3,)),
            dma((JOBS,)),
            dma((JOBS,)),
            dma((JOBS, 2)),
            dma((JOBS, 2)),
            dma((JOBS, 2)),
            dma((JOBS, 2)),
            dma((JOBS, 3)),
            dma((JOBS, 3)),
            dma((2,)),
            dma((2,)),
            dma((2, 2)),
            dma((2, 2)),
            dma((2, 2)),
            dma((2, 2)),
            dma((3,)),
            dma((3,)),
            dma,
            dma,
            dma((7,)),
            dma((7,)),
        ],
        compiler_params=pltpu.CompilerParams(
            collective_id=0, has_side_effects=True, vmem_limit_bytes=58 * 2**20
        ),
        cost_estimate=pl.CostEstimate(
            flops=15 * 10**9, bytes_accessed=8 * 10**6, transcendentals=2 * 10**6
        ),
        name="mla_backward",
    )(
        lengths,
        q_nope,
        q_rope,
        latent,
        k_rope.T,
        out_grad,
        w_key,
        w_value,
    )
    gq, gq_rope, g_latent, g_rope_t, g_wk, g_wv = pl.pallas_call(
        hand_over,
        out_shape=tuple(jax.ShapeDtypeStruct(array.shape, array.dtype) for array in out),
        in_specs=[vmem] * len(out),
        out_specs=[vmem] * len(out),
        name="hand_over",
    )(*out)
    return gq, gq_rope, g_latent, g_rope_t.T, g_wk, g_wv


def solution(mesh):
    placed = (
        P("ctx", "tp", None),
        P("ctx", "tp"),
        P("ctx", None),
        P("ctx", None),
        P("ctx", "tp", None),
        P("tp", None, None),
        P("tp", None, None),
        P(),
    )
    return jax.shard_map(
        per_device,
        mesh=mesh,
        in_specs=placed,
        out_specs=(
            P("ctx", "tp", None),
            P("ctx", "tp"),
            P("ctx", None),
            P("ctx", None),
            P("tp", "ctx", None),
            P("tp", "ctx", None),
        ),
        check_vma=False,
    )
```

time: 114 us -> 94.9 us (0.83)
  the two profiles are of different devices: /device:TPU:1 before, /device:TPU:2 now
where the time goes in v2:
time: 94.9 us; the launch traced here: 94.8 us
  Pallas kernels  94.2 us (99%)
    pallas_call x1, Pallas kernels, per_device(): pl.pallas_call(kernel, out_shape=(jax.ShapeDtypeStruct((TOK, HEADS, NOPE)...  92 us
    pallas_call x1, Pallas kernels, per_device(): pl.pallas_call(hand_over, out_shape=tuple((jax.ShapeDtypeStruct(array.sha...  2.14 us

profile of v2, /device:TPU:2, one launch (start us, length us, event | category | flops | bytes accessed | tf_op | source)
XLA Modules:
  0.0 94.8 jit_solution(11052777629541905669)
XLA Ops:
  0.6 92.0 %mla_backward.1 = (bf16[128,16,128]{2,1,0:T(8,128)(2,1)}, bf16[128,1024]{1,0:T(8,128)(2,1)}, bf16[128,512]{1,0:T(8,128)(2,1)}, bf16[64,128]{1,0:T(8,128)(2,1)}, ...) custom-call(s32[6]{0:T(128)} %lengths.1, bf16[128,16,128]{2,1,0:T(8,128)(2,1)} %q_hbm.1, ...), custom_call_target="tpu_custom_call" | custom-call | flops 15000000512 | bytes 8000000 | tf_op jit(solution)/shard_map/mla_backward/pallas_call | solution.py:637
  92.7 2.1 %hand_over.1 = (bf16[128,16,128]{2,1,0:T(8,128)(2,1)}, bf16[128,1024]{1,0:T(8,128)(2,1)}, bf16[128,512]{1,0:T(8,128)(2,1)}, bf16[64,128]{1,0:T(8,128)(2,1)}, bf1...) custom-call(bf16[128,16,128]{2,1,0:T(8,128)(2,1)} %get-tuple-element.18.refs_0_, ...), custom_call_target="tpu_custom_call" | custom-call | tf_op jit(solution)/shard_map/hand_over/pallas_call | solution.py:731

commit v3 on v2

--- a/solution.py
+++ b/solution.py
@@ -374,9 +374,13 @@
     def group(g, carry):
         cols = pl.ds(pl.multiple_of(g * COLS, COLS), COLS)
         s_buf[...] = nt(kw[...], q_all[cols, :])
-        @pl.when(g > 0)
+        @pl.when(g > 1)
         def _():
-            w_do1(g - 1)
+            w_do2(g - 2)
+
+        @pl.when(g > 2)
+        def _():
+            w_do3(g - 3, False)
 
         high = jnp.full((1, COLS), -jnp.inf, F32)
         for block in range(SPAN + 1):
@@ -399,7 +403,7 @@
 
         @pl.when(g > 0)
         def _():
-            w_do2(g - 1)
+            w_do1(g - 1)
 
         gp_buf[...] = nn(kw[:, :LATENT], gt_all[:, cols])
         out_t = nn(kwt[:LATENT, :], p_all[:, cols]).astype(BF16)
@@ -420,10 +424,6 @@
                             begin : begin + 16, :
                         ]
         w_stage0(g).start()
-
-        @pl.when(g > 0)
-        def _():
-            w_do3(g - 1, False)
 
         return carry
 
@@ -531,36 +531,43 @@
     for half in range(2):
         for quarter in range(4):
             kg[half, quarter, 7 * other] = jnp.zeros((16, WIDE), BF16)
-    w_do1(last)
+    w_do2(last - 1)
+    w_do3(last - 2, False)
     key_terms(0, 4)
     e0(0).start()
-    w_do2(last)
+    w_do1(last)
+    w_do3(last - 1, False)
     key_terms(4, 7)
     e0(1).start()
+    w_do2(last)
     k_do1(0)
     second(0)
     k_do1(1)
+    k_do2(0)
     w_do3(last, False)
-    k_do2(0)
     second(1)
+    w_do1(GROUPS)
     k_do2(1)
+    second(2)
+    w_do1(GROUPS + 1)
     k_do3(0)
-    w_do1(GROUPS)
-    second(2)
+    w_do2(GROUPS)
+    second(3)
     k_do3(1)
-    w_do2(GROUPS)
-    w_do1(GROUPS + 1)
-    second(3)
+    w_do1(GROUPS + 2)
+    w_do2(GROUPS + 1)
+    w_do3(GROUPS, True)
+    gq[...] = jnp.swapaxes(gq_t[...], 0, 1)
+    w_do1(GROUPS + 3)
+    w_do2(GROUPS + 2)
     for step in (1, 2, 3):
         e3(step).wait_recv()
     k_mid[...] = add(k_sum[6:8], k_r3[0], k_r3[1], k_r3[2]).astype(BF16)
     e4 = remote(k_mid, k_r4, e4_s, e4_r, place(zh_=1 - zh))
     e4.start()
-    w_do3(GROUPS, True)
-    w_do2(GROUPS + 1)
-    w_do1(GROUPS + 2)
-    w_do1(GROUPS + 3)
-    gq[...] = jnp.swapaxes(gq_t[...], 0, 1)
+    w_do3(GROUPS + 1, True)
+    w_do2(GROUPS + 3)
+    w_do3(GROUPS + 2, True)
     e4.wait_recv()
     total = add(k_mid[...], k_r4[...])
     k_fin[:, :, :LATENT] = total[:, :, :LATENT].astype(BF16)
@@ -589,12 +596,8 @@
     ]
     for copy in e5:
         copy.start()
-    w_do3(GROUPS + 1, True)
-    w_do2(GROUPS + 2)
-    w_do2(GROUPS + 3)
     for g in range(GROUPS):
         w_do4(g, False)
-    w_do3(GROUPS + 2, True)
     w_do3(GROUPS + 3, True)
     for copy in e5:
         copy.wait_recv()

time: 94.9 us -> 79.6 us (0.84)
  the two profiles are of different devices: /device:TPU:2 before, /device:TPU:1 now
where the time goes in v3:
time: 79.6 us; the launch traced here: 79.5 us
  Pallas kernels  78.9 us (99%)
    pallas_call x1, Pallas kernels, per_device(): pl.pallas_call(kernel, out_shape=(jax.ShapeDtypeStruct((TOK, HEADS, NOPE)...  76.7 us
    pallas_call x1, Pallas kernels, per_device(): pl.pallas_call(hand_over, out_shape=tuple((jax.ShapeDtypeStruct(array.sha...  2.14 us

profile of v3, /device:TPU:1, one launch (start us, length us, event | category | flops | bytes accessed | tf_op | source)
XLA Modules:
  0.0 79.5 jit_solution(16918321172114078467)
XLA Ops:
  0.6 76.7 %mla_backward.1 = (bf16[128,16,128]{2,1,0:T(8,128)(2,1)}, bf16[128,1024]{1,0:T(8,128)(2,1)}, bf16[128,512]{1,0:T(8,128)(2,1)}, bf16[64,128]{1,0:T(8,128)(2,1)}, ...) custom-call(s32[6]{0:T(128)} %lengths.1, bf16[128,16,128]{2,1,0:T(8,128)(2,1)} %q_hbm.1, ...), custom_call_target="tpu_custom_call" | custom-call | flops 15000000512 | bytes 8000000 | tf_op jit(solution)/shard_map/mla_backward/pallas_call | solution.py:640
  77.4 2.1 %hand_over.1 = (bf16[128,16,128]{2,1,0:T(8,128)(2,1)}, bf16[128,1024]{1,0:T(8,128)(2,1)}, bf16[128,512]{1,0:T(8,128)(2,1)}, bf16[64,128]{1,0:T(8,128)(2,1)}, bf1...) custom-call(bf16[128,16,128]{2,1,0:T(8,128)(2,1)} %get-tuple-element.18.refs_0_, ...), custom_call_target="tpu_custom_call" | custom-call | tf_op jit(solution)/shard_map/hand_over/pallas_call | solution.py:734

commit v4 on v3

--- a/solution.py
+++ b/solution.py
@@ -78,13 +78,11 @@
     w_out,
     w_r0,
     w_r1,
-    w_r2,
     w_v,
     w_rz,
     kg,
     k_r0,
     k_r1,
-    k_r2,
     k_sum,
     k_r3,
     k_mid,
@@ -104,16 +102,12 @@
     w0_r,
     w1_s,
     w1_r,
-    w2_s,
-    w2_r,
     wz_s,
     wz_r,
     e0_s,
     e0_r,
     e1_s,
     e1_r,
-    e2_s,
-    e2_r,
     e3_s,
     e3_r,
     e4_s,
@@ -141,13 +135,11 @@
         return (lax.rem(chip + step + 16, 16) * 2 + core, tp)
 
     sibling = place(core_=other)
-    x_next, x_prev, x_far = up(x, 1), up(x, 3), up(x, 2)
-    y_next, y_prev, y_far = up(y, 1), up(y, 3), up(y, 2)
 
     barrier = pltpu.get_barrier_semaphore()
-    peers = [sibling, place(x_=x_next), place(x_=x_prev), place(zh_=1 - zh)]
+    peers = [sibling, place(zh_=1 - zh)]
     for step in (1, 2, 3):
-        peers += [place(z_=up(z, step)), chip_at(step), chip_at(-step)]
+        peers += [place(x_=up(x, step)), place(z_=up(z, step)), chip_at(step), chip_at(-step)]
         peers += [place(y_=up(y, step)), place(y_=up(y, step), core_=other)]
     for peer in peers:
         pl.semaphore_signal(barrier, inc=1, device_id=peer, device_id_type=MESH)
@@ -275,42 +267,18 @@
         return remote(w_out.at[g, other], w_r0.at[g], w0_s.at[g], w0_r.at[g], sibling)
 
     def w_stage1(g):
-        return (
+        return [
             remote(
-                w_out.at[g, core, x_far, pl.ds(0, 32)],
-                w_r1.at[g, 0],
-                w1_s.at[g, 0],
-                w1_r.at[g, 0],
-                place(x_=x_next),
-            ),
-            remote(
-                w_out.at[g, core, x_far, pl.ds(32, 32)],
-                w_r1.at[g, 1],
-                w1_s.at[g, 1],
-                w1_r.at[g, 1],
-                place(x_=x_prev),
-            ),
-        )
+                w_out.at[g, core, up(x, step)],
+                w_r1.at[g, step - 1],
+                w1_s.at[g, step - 1],
+                w1_r.at[g, step - 1],
+                place(x_=up(x, step)),
+            )
+            for step in (2, 1, 3)
+        ]
 
     def w_stage2(g):
-        return (
-            remote(
-                w_out.at[g, core, x_next],
-                w_r2.at[g, 0],
-                w2_s.at[g, 0],
-                w2_r.at[g, 0],
-                place(x_=x_next),
-            ),
-            remote(
-                w_out.at[g, core, x_prev],
-                w_r2.at[g, 1],
-                w2_s.at[g, 1],
-                w2_r.at[g, 1],
-                place(x_=x_prev),
-            ),
-        )
-
-    def w_stage3(g):
         return [
             remote(
                 w_v.at[g, up(z, step)],
@@ -333,21 +301,10 @@
         for copy in w_stage1(g):
             copy.start()
 
-    def w_do2(g):
-        first, second = w_stage1(g)
-        first.wait_recv()
-        low = w_out[g, core, x_next, 0:32, :]
-        w_out[g, core, x_next, 0:32, :] = add(low, w_r1[g, 0]).astype(BF16)
-        second.wait_recv()
-        high = w_out[g, core, x_prev, 32:64, :]
-        w_out[g, core, x_prev, 32:64, :] = add(high, w_r1[g, 1]).astype(BF16)
-        for copy in w_stage2(g):
-            copy.start()
-
-    def w_do3(g, of_key):
-        for copy in w_stage2(g):
+    def w_do2(g, of_key):
+        for copy in w_stage1(g):
             copy.wait_recv()
-        total = add(w_out[g, core, x], w_r2[g, 0], w_r2[g, 1]).astype(BF16)
+        total = add(w_out[g, core, x], w_r1[g, 0], w_r1[g, 1], w_r1[g, 2]).astype(BF16)
         if of_key:
             total = nn(by_z, total).astype(BF16)
             for part in range(4):
@@ -358,11 +315,11 @@
                     w_v[g, part, :, head * 128 : head * 128 + 128] = total[
                         head * 16 : head * 16 + 16, part * 128 : part * 128 + 128
                     ]
-        for copy in w_stage3(g):
+        for copy in w_stage2(g):
             copy.start()
 
-    def w_do4(g, of_key):
-        for copy in w_stage3(g):
+    def w_do3(g, of_key):
+        for copy in w_stage2(g):
             copy.wait_recv()
         total = add(w_v[g, z], w_rz[g, 0], w_rz[g, 1], w_rz[g, 2]).astype(BF16)
         for local in range(PACK):
@@ -374,14 +331,6 @@
     def group(g, carry):
         cols = pl.ds(pl.multiple_of(g * COLS, COLS), COLS)
         s_buf[...] = nt(kw[...], q_all[cols, :])
-        @pl.when(g > 1)
-        def _():
-            w_do2(g - 2)
-
-        @pl.when(g > 2)
-        def _():
-            w_do3(g - 3, False)
-
         high = jnp.full((1, COLS), -jnp.inf, F32)
         for block in range(SPAN + 1):
             rows = slice(block * TOK, (block + 1) * TOK)
@@ -424,6 +373,10 @@
                             begin : begin + 16, :
                         ]
         w_stage0(g).start()
+
+        @pl.when(g > 1)
+        def _():
+            w_do2(g - 2, False)
 
         return carry
 
@@ -451,9 +404,10 @@
     lax.fori_loop(0, GROUPS, group, 0)
     last = GROUPS - 1
 
-    def key_terms(first, after):
+    def key_terms(first, after, between):
         rows = slice(first * TOK, after * TOK)
         wide = nn(ds_all[rows, :], q_all[...])
+        between()
         narrow = wide[:, :LATENT] + nt(p_all[rows, :], gt_all[...])
         narrow, side = narrow.astype(BF16), wide[:, LATENT:].astype(BF16)
         for block in range(first, after):
@@ -470,27 +424,16 @@
         )
 
     def e1(n):
+        blocks = pl.ds(4 * n, 4)
         return [
             remote(
-                kg.at[core, y_far, pl.ds(4 * n + 2 * way, 2)],
-                k_r1.at[n, way],
-                e1_s.at[n, way],
-                e1_r.at[n, way],
-                place(y_=y_to),
+                kg.at[core, up(y, step), blocks],
+                k_r1.at[n, step - 1],
+                e1_s.at[n, step - 1],
+                e1_r.at[n, step - 1],
+                place(y_=up(y, step)),
             )
-            for way, y_to in ((0, y_next), (1, y_prev))
-        ]
-
-    def e2(n):
-        return [
-            remote(
-                kg.at[core, y_to, pl.ds(4 * n, 4)],
-                k_r2.at[n, way],
-                e2_s.at[n, way],
-                e2_r.at[n, way],
-                place(y_=y_to),
-            )
-            for way, y_to in ((0, y_next), (1, y_prev))
+            for step in (2, 1, 3)
         ]
 
     def e3(step):
@@ -513,61 +456,45 @@
             copy.start()
 
     def k_do2(n):
-        for way, (copy, y_to) in enumerate(zip(e1(n), (y_next, y_prev))):
-            copy.wait_recv()
-            blocks = slice(4 * n + 2 * way, 4 * n + 2 * way + 2)
-            kg[core, y_to, blocks] = add(kg[core, y_to, blocks], k_r1[n, way]).astype(BF16)
-        for copy in e2(n):
-            copy.start()
-
-    def k_do3(n):
-        for copy in e2(n):
+        for copy in e1(n):
             copy.wait_recv()
         blocks = slice(4 * n, 4 * n + 4)
-        k_sum[blocks] = add(kg[core, y, blocks], k_r2[n, 0], k_r2[n, 1]).astype(BF16)
+        k_sum[blocks] = add(kg[core, y, blocks], k_r1[n, 0], k_r1[n, 1], k_r1[n, 2]).astype(BF16)
         for step in ((3, 2), (1,))[n]:
             e3(step).start()
 
     for half in range(2):
         for quarter in range(4):
             kg[half, quarter, 7 * other] = jnp.zeros((16, WIDE), BF16)
-    w_do2(last - 1)
-    w_do3(last - 2, False)
-    key_terms(0, 4)
+    key_terms(0, 4, lambda: w_do1(last))
     e0(0).start()
-    w_do1(last)
-    w_do3(last - 1, False)
-    key_terms(4, 7)
+    key_terms(4, 7, lambda: k_do1(0))
     e0(1).start()
-    w_do2(last)
-    k_do1(0)
+    w_do2(last - 1, False)
     second(0)
     k_do1(1)
-    k_do2(0)
-    w_do3(last, False)
     second(1)
     w_do1(GROUPS)
+    w_do2(last, False)
+    second(2)
+    k_do2(0)
+    w_do1(GROUPS + 1)
+    second(3)
     k_do2(1)
-    second(2)
-    w_do1(GROUPS + 1)
-    k_do3(0)
-    w_do2(GROUPS)
-    second(3)
-    k_do3(1)
     w_do1(GROUPS + 2)
-    w_do2(GROUPS + 1)
-    w_do3(GROUPS, True)
     gq[...] = jnp.swapaxes(gq_t[...], 0, 1)
     w_do1(GROUPS + 3)
-    w_do2(GROUPS + 2)
+    w_do2(GROUPS, True)
     for step in (1, 2, 3):
         e3(step).wait_recv()
     k_mid[...] = add(k_sum[6:8], k_r3[0], k_r3[1], k_r3[2]).astype(BF16)
     e4 = remote(k_mid, k_r4, e4_s, e4_r, place(zh_=1 - zh))
     e4.start()
-    w_do3(GROUPS + 1, True)
-    w_do2(GROUPS + 3)
-    w_do3(GROUPS + 2, True)
+    w_do2(GROUPS + 1, True)
+    w_do2(GROUPS + 2, True)
+    w_do2(GROUPS + 3, True)
+    for g in range(GROUPS):
+        w_do3(g, False)
     e4.wait_recv()
     total = add(k_mid[...], k_r4[...])
     k_fin[:, :, :LATENT] = total[:, :, :LATENT].astype(BF16)
@@ -596,9 +523,6 @@
     ]
     for copy in e5:
         copy.start()
-    for g in range(GROUPS):
-        w_do4(g, False)
-    w_do3(GROUPS + 3, True)
     for copy in e5:
         copy.wait_recv()
     for quarter in range(4):
@@ -607,19 +531,19 @@
             g_latent[begin : begin + 16, :] = k_out[quarter, half, :, :LATENT]
     g_rope_t[...] = k_out[:, :, :, LATENT:].reshape(TOK, 2 * ROPE).T[:ROPE, :]
     for g in range(GROUPS, JOBS):
-        w_do4(g, True)
+        w_do3(g, True)
 
     own.wait_send()
     e4.wait_send()
     for n in range(2):
-        for copy in [e0(n), *e1(n), *e2(n)]:
+        for copy in [e0(n), *e1(n)]:
             copy.wait_send()
     for copy in [*ahead, *across, *e5, *(copy for three in around for copy in three)]:
         copy.wait_send()
     for step in (1, 2, 3):
         e3(step).wait_send()
     for g in range(JOBS):
-        for copy in [w_stage0(g), *w_stage1(g), *w_stage2(g), *w_stage3(g)]:
+        for copy in [w_stage0(g), *w_stage1(g), *w_stage2(g)]:
             copy.wait_send()
 
 
@@ -670,14 +594,12 @@
             held(WINDOW, TOK, dtype=F32),
             held(JOBS, 2, 4, 64, LATENT),
             held(JOBS, 4, 64, LATENT),
-            held(JOBS, 2, 32, LATENT),
-            held(JOBS, 2, 64, LATENT),
+            held(JOBS, 3, 64, LATENT),
             held(JOBS, 4, 16, LATENT),
             held(JOBS, 3, 16, LATENT),
             held(2, 4, 8, 16, WIDE),
             held(4, 8, 16, WIDE),
-            held(2, 2, 2, 16, WIDE),
-            held(2, 2, 4, 16, WIDE),
+            held(2, 3, 4, 16, WIDE),
             held(8, 16, WIDE),
             held(3, 2, 16, WIDE),
             held(2, 16, WIDE),
@@ -695,18 +617,14 @@
             dma((3,)),
             dma((JOBS,)),
             dma((JOBS,)),
-            dma((JOBS, 2)),
-            dma((JOBS, 2)),
-            dma((JOBS, 2)),
-            dma((JOBS, 2)),
+            dma((JOBS, 3)),
+            dma((JOBS, 3)),
             dma((JOBS, 3)),
             dma((JOBS, 3)),
             dma((2,)),
             dma((2,)),
-            dma((2, 2)),
-            dma((2, 2)),
-            dma((2, 2)),
-            dma((2, 2)),
+            dma((2, 3)),
+            dma((2, 3)),
             dma((3,)),
             dma((3,)),
             dma,

time: 79.6 us -> 73.4 us (0.922)
  Pallas kernels: 78.9 us -> 72.7 us
    pallas_call x1, Pallas kernels: 76.7 us -> 70.5 us  [per_device(): pl.pallas_call(kernel, out_shape=(jax.ShapeDtypeStruct((TOK, HEADS, NOPE)...]
where the time goes in v4:
time: 73.4 us; the launch traced here: 73.3 us
  Pallas kernels  72.7 us (99%)
    pallas_call x1, Pallas kernels, per_device(): pl.pallas_call(kernel, out_shape=(jax.ShapeDtypeStruct((TOK, HEADS, NOPE)...  70.5 us
    pallas_call x1, Pallas kernels, per_device(): pl.pallas_call(hand_over, out_shape=tuple((jax.ShapeDtypeStruct(array.sha...  2.14 us

profile of v4, /device:TPU:1, one launch (start us, length us, event | category | flops | bytes accessed | tf_op | source)
XLA Modules:
  0.0 73.3 jit_solution(7199271024116030915)
XLA Ops:
  0.6 70.5 %mla_backward.1 = (bf16[128,16,128]{2,1,0:T(8,128)(2,1)}, bf16[128,1024]{1,0:T(8,128)(2,1)}, bf16[128,512]{1,0:T(8,128)(2,1)}, bf16[64,128]{1,0:T(8,128)(2,1)}, ...) custom-call(s32[6]{0:T(128)} %lengths.1, bf16[128,16,128]{2,1,0:T(8,128)(2,1)} %q_hbm.1, ...), custom_call_target="tpu_custom_call" | custom-call | flops 15000000512 | bytes 8000000 | tf_op jit(solution)/shard_map/mla_backward/pallas_call | solution.py:564
  71.2 2.1 %hand_over.1 = (bf16[128,16,128]{2,1,0:T(8,128)(2,1)}, bf16[128,1024]{1,0:T(8,128)(2,1)}, bf16[128,512]{1,0:T(8,128)(2,1)}, bf16[64,128]{1,0:T(8,128)(2,1)}, bf1...) custom-call(bf16[128,16,128]{2,1,0:T(8,128)(2,1)} %get-tuple-element.18.refs_0_, ...), custom_call_target="tpu_custom_call" | custom-call | tf_op jit(solution)/shard_map/hand_over/pallas_call | solution.py:652

commit v5 on v4

--- a/solution.py
+++ b/solution.py
@@ -65,6 +65,9 @@
     og,
     qt,
     gq_t,
+    gq_v,
+    gqr_v,
+    dq_all,
     kall,
     kw,
     kwt,
@@ -90,6 +93,7 @@
     k_fin,
     k_out,
     load_s,
+    leave_s,
     own_s,
     own_r,
     ctx_s,
@@ -225,7 +229,7 @@
                     yag_r.at[near - 1, step - 1],
                     place(y_=up(y, step)),
                 )
-                for step in (1, 2, 3)
+                for step in (2, 1, 3)
             ]
         )
         for copy in around[-1]:
@@ -246,6 +250,13 @@
         allowed = (key_pos >= doc_start) & (key_pos <= query_pos)
         bias[block * TOK : (block + 1) * TOK, :] = jnp.where(allowed, 0.0, -jnp.inf).astype(F32)
 
+    def place_keys(block):
+        at = core + block
+        keys = kall[lax.div(at, 2), lax.rem(at, 2)].reshape(TOK, WIDE)
+        kw[block * TOK : (block + 1) * TOK, :] = keys
+        kwt[:, block * TOK : (block + 1) * TOK] = keys.T
+
+    place_keys(6)
     across = []
     for near in (1, 2, 3):
         for copy in around[near - 1]:
@@ -254,14 +265,10 @@
         across.append(remote(part, part, sib_s.at[near - 1], sib_r.at[near - 1], sibling))
         across[-1].start()
     own.wait_recv()
-    for copy in across:
-        copy.wait_recv()
-
-    for block in range(SPAN + 1):
-        at = core + block
-        keys = kall[lax.div(at, 2), lax.rem(at, 2)].reshape(TOK, WIDE)
-        kw[block * TOK : (block + 1) * TOK, :] = keys
-        kwt[:, block * TOK : (block + 1) * TOK] = keys.T
+    for near in (1, 2, 3):
+        across[near - 1].wait_recv()
+        place_keys(7 - 2 * near)
+        place_keys(6 - 2 * near)
 
     def w_stage0(g):
         return remote(w_out.at[g, other], w_r0.at[g], w0_s.at[g], w0_r.at[g], sibling)
@@ -380,26 +387,29 @@
 
         return carry
 
-    def second(g):
+    def query_terms(g):
         cols = slice(g * COLS, (g + 1) * COLS)
-        dq_t = nn(kwt[...], ds_all[:, cols]).astype(BF16)
+        dq_all[g] = nn(kwt[...], ds_all[:, cols]).astype(BF16)
         for local in range(PACK):
-            head = g * PACK + local
-            here = slice(local * TOK, (local + 1) * TOK)
-            mine = dq_t[:LATENT, here]
-            gq_t[head] = nt(eye, nn(wk[head], mine).astype(BF16)).astype(BF16)
-            gwk = nt(qt[head], mine).astype(BF16)
+            mine = dq_all[g, :LATENT, local * TOK : (local + 1) * TOK]
+            gwk = nt(qt[g * PACK + local], mine).astype(BF16)
             rows = slice(local * 16, local * 16 + 16)
             for half in range(2):
                 for part in range(4):
                     begin = half * 64 + part * 16
                     w_out[GROUPS + g, half, part, rows, :] = gwk[begin : begin + 16, :]
+        w_stage0(GROUPS + g).start()
+
+    def query_out(g):
+        for local in range(PACK):
+            head = g * PACK + local
+            mine = dq_all[g, :LATENT, local * TOK : (local + 1) * TOK]
+            gq_t[head] = nt(eye, nn(wk[head], mine).astype(BF16)).astype(BF16)
         for pair in range(PACK // 2):
-            left = dq_t[LATENT : LATENT + ROPE, pair * 256 : pair * 256 + 128]
-            right = dq_t[LATENT + ROPE :, pair * 256 + 128 : pair * 256 + 256]
+            left = dq_all[g, LATENT : LATENT + ROPE, pair * 256 : pair * 256 + 128]
+            right = dq_all[g, LATENT + ROPE :, pair * 256 + 128 : pair * 256 + 256]
             both = nt(eye, jnp.concatenate([left, right], axis=0)).astype(BF16)
-            gq_rope[:, (g * 2 + pair) * 128 : (g * 2 + pair + 1) * 128] = both
-        w_stage0(GROUPS + g).start()
+            gqr_v[:, (g * 2 + pair) * 128 : (g * 2 + pair + 1) * 128] = both
 
     lax.fori_loop(0, GROUPS, group, 0)
     last = GROUPS - 1
@@ -471,28 +481,37 @@
     key_terms(4, 7, lambda: k_do1(0))
     e0(1).start()
     w_do2(last - 1, False)
-    second(0)
+    query_terms(0)
     k_do1(1)
-    second(1)
+    query_terms(1)
     w_do1(GROUPS)
     w_do2(last, False)
-    second(2)
+    query_terms(2)
+    w_do1(GROUPS + 1)
+    query_terms(3)
+    w_do1(GROUPS + 2)
+    query_out(0)
     k_do2(0)
-    w_do1(GROUPS + 1)
-    second(3)
+    w_do1(GROUPS + 3)
+    query_out(1)
+    query_out(2)
     k_do2(1)
-    w_do1(GROUPS + 2)
-    gq[...] = jnp.swapaxes(gq_t[...], 0, 1)
-    w_do1(GROUPS + 3)
     w_do2(GROUPS, True)
+    query_out(3)
+    gq_v[...] = jnp.swapaxes(gq_t[...], 0, 1)
+    leave = [
+        pltpu.make_async_copy(gq_v, gq, leave_s.at[0]),
+        pltpu.make_async_copy(gqr_v, gq_rope, leave_s.at[1]),
+    ]
+    for copy in leave:
+        copy.start()
+    w_do2(GROUPS + 1, True)
     for step in (1, 2, 3):
         e3(step).wait_recv()
     k_mid[...] = add(k_sum[6:8], k_r3[0], k_r3[1], k_r3[2]).astype(BF16)
     e4 = remote(k_mid, k_r4, e4_s, e4_r, place(zh_=1 - zh))
     e4.start()
-    w_do2(GROUPS + 1, True)
     w_do2(GROUPS + 2, True)
-    w_do2(GROUPS + 3, True)
     for g in range(GROUPS):
         w_do3(g, False)
     e4.wait_recv()
@@ -523,6 +542,9 @@
     ]
     for copy in e5:
         copy.start()
+    w_do2(GROUPS + 3, True)
+    w_do3(GROUPS, True)
+    w_do3(GROUPS + 1, True)
     for copy in e5:
         copy.wait_recv()
     for quarter in range(4):
@@ -530,8 +552,10 @@
             begin = quarter * 32 + half * 16
             g_latent[begin : begin + 16, :] = k_out[quarter, half, :, :LATENT]
     g_rope_t[...] = k_out[:, :, :, LATENT:].reshape(TOK, 2 * ROPE).T[:ROPE, :]
-    for g in range(GROUPS, JOBS):
-        w_do3(g, True)
+    w_do3(GROUPS + 2, True)
+    w_do3(GROUPS + 3, True)
+    for copy in leave:
+        copy.wait()
 
     own.wait_send()
     e4.wait_send()
@@ -572,7 +596,7 @@
             jax.ShapeDtypeStruct((HEADS, 16, NOPE), BF16),
         ),
         in_specs=[pl.BlockSpec(memory_space=pltpu.SMEM), hbm, hbm, vmem, vmem, hbm, hbm, hbm],
-        out_specs=[vmem] * 6,
+        out_specs=[hbm] * 2 + [vmem] * 4,
         scratch_shapes=[
             held(TOK, HEADS, NOPE),
             held(TOK, HEADS, NOPE),
@@ -582,6 +606,9 @@
             held(HEADS, TOK, NOPE),
             held(HEADS, NOPE, TOK),
             held(HEADS, TOK, NOPE),
+            held(TOK, HEADS, NOPE),
+            held(TOK, HEADS * ROPE),
+            held(GROUPS, WIDE, COLS),
             held(4, 2, 4, 32, WIDE),
             held(WINDOW, WIDE),
             held(WIDE, WINDOW),
@@ -607,6 +634,7 @@
             held(2, 16, WIDE),
             held(4, 2, 16, WIDE),
             dma((5,)),
+            dma((2,)),
             dma,
             dma,
             dma((3,)),

time: 73.4 us -> 72.2 us (0.984)
  Pallas kernels: 72.7 us -> 71.4 us
    pallas_call x1, Pallas kernels: 70.5 us -> 69.2 us  [per_device(): pl.pallas_call(kernel, out_shape=(jax.ShapeDtypeStruct((TOK, HEADS, NOPE)...]
where the time goes in v5:
time: 72.2 us; the launch traced here: 72 us
  Pallas kernels  71.4 us (99%)
    pallas_call x1, Pallas kernels, per_device(): pl.pallas_call(kernel, out_shape=(jax.ShapeDtypeStruct((TOK, HEADS, NOPE)...  69.2 us
    pallas_call x1, Pallas kernels, per_device(): pl.pallas_call(hand_over, out_shape=tuple((jax.ShapeDtypeStruct(array.sha...  2.14 us

profile of v5, /device:TPU:1, one launch (start us, length us, event | category | flops | bytes accessed | tf_op | source)
XLA Modules:
  0.0 72.0 jit_solution(17754973770641055819)
XLA Ops:
  0.6 69.2 %mla_backward.1 = (bf16[128,16,128]{2,1,0:T(8,128)(2,1)}, bf16[128,1024]{1,0:T(8,128)(2,1)}, bf16[128,512]{1,0:T(8,128)(2,1)}, bf16[64,128]{1,0:T(8,128)(2,1)}, ...) custom-call(s32[6]{0:T(128)} %lengths.1, bf16[128,16,128]{2,1,0:T(8,128)(2,1)} %q_hbm.1, ...), custom_call_target="tpu_custom_call" | custom-call | flops 15000000512 | bytes 8000000 | tf_op jit(solution)/shard_map/mla_backward/pallas_call | solution.py:588
  69.9 2.1 %hand_over.1 = (bf16[128,16,128]{2,1,0:T(8,128)(2,1)}, bf16[128,1024]{1,0:T(8,128)(2,1)}, bf16[128,512]{1,0:T(8,128)(2,1)}, bf16[64,128]{1,0:T(8,128)(2,1)}, bf1...) custom-call(bf16[128,16,128]{2,1,0:T(8,128)(2,1)} %get-tuple-element.18.refs_0_, ...), custom_call_target="tpu_custom_call" | custom-call | tf_op jit(solution)/shard_map/hand_over/pallas_call | solution.py:680
